TPU v7x, 128 devices: a whole 4x4x4 slice. The times are simulated.
128 devices in a mesh: lev: 2 (over x_lo), lat: 64 (over y, z, x_hi, core).
Axes of the slice: x: 4 (x_hi: 2, x_lo: 2; x = x_hi * 2 + x_lo), y: 4, z: 4, core: 2. Of those that a mesh axis runs over, the one named last changes fastest.
Arguments:
- tokens: bfloat16 [8, 384, 24, 512], P('lev', 'lat'), may hold values from -6 to 6
- level_ids: int32 [8], P('lev'), may hold values from 0 to 12
- level_table: float32 [13, 512], replicated, may hold values from -6 to 6
- latent_query: bfloat16 [4, 512], replicated, may hold values from -360 to 360
- w_query: bfloat16 [512, 512], replicated, may hold values from -0.25 to 0.25
- w_kv: bfloat16 [512, 1024], replicated, may hold values from -0.25 to 0.25
- w_attn_out: bfloat16 [512, 512], replicated, may hold values from -0.25 to 0.25
- regions: int32 [384, 24, 4], P('lat', 'lev'), may hold values from 0 to 3
- gain_one: float32 [2, 512], replicated, may hold values from 0.25 to 1.75
- gain_two: float32 [2, 512], replicated, may hold values from 0.25 to 1.75
- w_qkv: bfloat16 [2, 512, 1536], P(None, 'lat'), may hold values from -0.25 to 0.25
- w_proj: bfloat16 [2, 512, 512], P(None, 'lat'), may hold values from -0.25 to 0.25
- w_up: bfloat16 [2, 512, 2048], P(None, 'lat'), may hold values from -0.25 to 0.25
- w_down: bfloat16 [2, 2048, 512], P(None, 'lat'), may hold values from -0.125 to 0.125
Outputs:
- grid_out: bfloat16 [384, 24, 4, 512], P('lat', 'lev')
Inputs may be any that keep to these rules, and one draw needn't show every extreme that they name: `regions`: within a window of the shifted grid, tokens attend only to tokens of the same region id.
All inputs are finite; a program needn't handle non-finite values.
Results may differ from a plain program's by a relative error of at most 0.018.
Values may be sent and summed in bfloat16 or wider, within the bound.
A program may use at most 64 MiB of HBM per device.

v0:
```python
import jax
import jax.numpy as jnp
from jax import lax
from jax.sharding import PartitionSpec as P

HEADS = 16
HD = 32
Q_LAT = 4
COLS_DEV = 12
BLOCKS = 2


eps = 1e-05


def joined_along(pieces, dim):
    pieces = jnp.moveaxis(pieces, 0, dim)
    shape = pieces.shape
    return pieces.reshape(*shape[:dim], shape[dim] * shape[dim + 1], *shape[dim + 2 :])


def gather_packed(arrays, axis, dims):
    flat = jnp.concatenate([a.reshape(-1) for a in arrays])
    lines, at, outs = (lax.all_gather(flat, axis), 0, [])
    for a, dim in zip(arrays, dims):
        pieces = lines[:, at : at + a.size].reshape(-1, *a.shape)
        outs.append(joined_along(pieces, dim))
        at += a.size
    return tuple(outs)


def from_behind(block, axis, distance):
    devices = range(lax.axis_size(axis))
    route = [((i - distance) % len(devices), i) for i in devices]
    return lax.ppermute(block, axis, route)


def partner(array, axis, apart):
    return lax.ppermute(array, axis, [(i, i ^ 1 << apart) for i in range(lax.axis_size(axis))])


def layer_norm(flat, gain):
    mean = jnp.mean(flat, -1, keepdims=True)
    centred = flat - mean
    var = jnp.mean(centred * centred, -1, keepdims=True)
    return centred * lax.rsqrt(var + eps) * gain


def windows(grid):
    rows, cols, levels, width = grid.shape
    grid = grid.reshape(rows // 6, 6, cols // 12, 12, levels // 2, 2, width)
    grid = grid.transpose(0, 2, 4, 1, 3, 5, 6)
    return grid.reshape(-1, 144, width)


def unwindows(tiles, rows, cols, levels):
    width = tiles.shape[-1]
    tiles = tiles.reshape(rows // 6, cols // 12, levels // 2, 6, 12, 2, width)
    tiles = tiles.transpose(0, 3, 1, 4, 2, 5, 6)
    return tiles.reshape(rows, cols, levels, width)


def level_embed(level_ids, level_table):
    kinds = level_table.shape[0]
    onehot = (level_ids[:, None] == jnp.arange(kinds, dtype=jnp.int32)[None, :]).astype(jnp.float32)
    return jnp.dot(onehot, level_table, precision=lax.Precision.HIGHEST)


def head_spread(width):
    owner = jnp.arange(width, dtype=jnp.int32) // HD
    return (owner[None, :] == jnp.arange(HEADS, dtype=jnp.int32)[:, None]).astype(jnp.float32)


def expand_heads(values, spread):
    shape = values.shape[:-1]
    wide = jnp.dot(values.reshape(-1, HEADS), spread, precision=lax.Precision.HIGHEST)
    return wide.reshape(shape + (Q_LAT, spread.shape[1]))


def partials(summed, w_kv, query_block, spread):
    slots, rows, cols, width = summed.shape
    kv = jnp.dot(summed.reshape(-1, width), w_kv, preferred_element_type=jnp.float32).astype(
        jnp.bfloat16
    )
    keys = kv[:, :width]
    values = kv[:, width:].reshape(slots, rows, cols, 1, width)
    score = jnp.dot(keys, query_block, preferred_element_type=jnp.float32) * HD ** (-0.5)
    score = score.reshape(slots, rows, cols, Q_LAT * HEADS)
    top = jnp.max(score, 0)
    weight = jnp.exp(score - top[None])
    total = jnp.sum(weight, 0)
    wide = expand_heads(weight, spread)
    accum = jnp.sum(wide * values.astype(jnp.float32), 0)
    return (top, total, accum)


def swin_block(grid, regions, gain_a, gain_b, w_qkv, w_proj, w_up, w_down, masked, spread):
    rows, cols, levels, width = grid.shape
    tiled = windows(grid)
    count = tiled.shape[0]
    groups = rows // 6
    per_group = count // groups
    flat = tiled.reshape(-1, width).astype(jnp.float32)
    normed = layer_norm(flat, gain_a).astype(jnp.bfloat16)
    qkv = jnp.dot(normed, w_qkv, preferred_element_type=jnp.float32).astype(jnp.bfloat16)
    qkv = qkv.reshape(groups, per_group, 144, 3 * width)
    if masked:
        idents = windows(regions[..., None])[..., 0].reshape(groups, per_group, 144)
    else:
        idents = jnp.zeros((groups, per_group, 144), jnp.int32)
    select = spread.astype(jnp.bfloat16)

    def attend(pair):
        block, labels = pair
        query = block[..., :width]
        keys = block[..., width : 2 * width]
        vals = block[..., 2 * width :]
        per_head = query[:, None] * select[None, :, None, :]
        score = jnp.einsum(
            "nhad,nbd->nhab", per_head, keys, preferred_element_type=jnp.float32
        ) * HD ** (-0.5)
        if masked:
            same = labels[:, :, None] == labels[:, None, :]
            score = jnp.where(same[:, None], score, -1000000000.0)
        top = jnp.max(score, -1, keepdims=True)
        weight = jnp.exp(score - top)
        weight = (weight / jnp.sum(weight, -1, keepdims=True)).astype(jnp.bfloat16)
        output = jnp.einsum("nhab,nbd->nhad", weight, vals, preferred_element_type=jnp.float32)
        return jnp.sum(output * spread[None, :, None, :], 1).astype(jnp.bfloat16)

    context = lax.map(attend, (qkv, idents)).reshape(-1, width)
    mixed = (flat + jnp.dot(context, w_proj, preferred_element_type=jnp.float32)).astype(
        jnp.bfloat16
    )
    normed_b = layer_norm(mixed.astype(jnp.float32), gain_b).astype(jnp.bfloat16)
    hidden = jax.nn.gelu(jnp.dot(normed_b, w_up, preferred_element_type=jnp.float32)).astype(
        jnp.bfloat16
    )
    result = (
        mixed.astype(jnp.float32) + jnp.dot(hidden, w_down, preferred_element_type=jnp.float32)
    ).astype(jnp.bfloat16)
    return unwindows(result.reshape(count, 144, width), rows, cols, levels)


def block_weights(stacked, index):
    shard = tuple((weight[index] for weight in stacked))
    return gather_packed((shard[0], shard[1], shard[2], shard[3]), "lat", (0, 0, 0, 0))


def move_rows(grid, sign):
    edge = grid[:3] if sign < 0 else grid[-3:]
    moved = from_behind(edge, "lat", sign)
    if sign < 0:
        return jnp.concatenate([grid[3:], moved], 0)
    return jnp.concatenate([moved, grid[:-3]], 0)


def move_cols(grid, sign):
    edge = grid[:, :6] if sign < 0 else grid[:, -6:]
    moved = partner(edge, "lev", 0)
    if sign < 0:
        return jnp.concatenate([grid[:, 6:], moved], 1)
    return jnp.concatenate([moved, grid[:, :-6]], 1)


def roll_tile(grid, sign):
    return move_cols(move_rows(grid, sign), sign)


def local(
    tokens,
    level_ids,
    level_table,
    latent_query,
    w_query,
    w_kv,
    w_attn_out,
    regions,
    gain_one,
    gain_two,
    w_qkv,
    w_proj,
    w_up,
    w_down,
):
    slots, rows, cols_all, width = tokens.shape
    spread = head_spread(width)
    embed = level_embed(level_ids, level_table)
    summed = (tokens.astype(jnp.float32) + embed[:, None, None, :]).astype(jnp.bfloat16)
    queries = jnp.dot(latent_query, w_query, preferred_element_type=jnp.float32).astype(
        jnp.bfloat16
    )
    query_block = (
        (queries[:, None, :] * spread.astype(jnp.bfloat16)[None]).reshape(Q_LAT * HEADS, width).T
    )
    gathered = lax.all_to_all(summed, "lev", split_axis=2, concat_axis=0, tiled=True)
    top, total, accum = partials(gathered, w_kv, query_block, spread)
    attended = (accum / expand_heads(total, spread)).astype(jnp.bfloat16).reshape(-1, width)
    projected = jnp.dot(attended, w_attn_out, preferred_element_type=jnp.float32).reshape(
        rows, COLS_DEV, Q_LAT, width
    )
    state = (projected + queries.astype(jnp.float32)).astype(jnp.bfloat16)
    stacked = (w_qkv, w_proj, w_up, w_down)
    for index in range(BLOCKS):
        weights = block_weights(stacked, index)
        if index % 2 == 0:
            state = swin_block(
                state,
                regions,
                gain_one[index],
                gain_two[index],
                weights[0],
                weights[1],
                weights[2],
                weights[3],
                False,
                spread,
            )
        else:
            rolled = roll_tile(jnp.roll(state, -1, 2), -1)
            shifted = swin_block(
                rolled,
                regions,
                gain_one[index],
                gain_two[index],
                weights[0],
                weights[1],
                weights[2],
                weights[3],
                True,
                spread,
            )
            state = jnp.roll(roll_tile(shifted, 1), 1, 2)
    return state


def solution(mesh):
    in_specs = (
        P("lev", "lat", None, None),
        P("lev"),
        P(),
        P(),
        P(),
        P(),
        P(),
        P("lat", "lev", None),
        P(),
        P(),
        P(None, "lat", None),
        P(None, "lat", None),
        P(None, "lat", None),
        P(None, "lat", None),
    )
    out_specs = P("lat", "lev", None, None)
    return jax.shard_map(local, mesh=mesh, in_specs=in_specs, out_specs=out_specs, check_vma=False)
```

profile of v0, /device:TPU:0, one launch (start us, length us, event | category | flops | bytes accessed | tf_op | source)
XLA Modules:
  0.0 231.1 jit_solution(5535684637199217421)
XLA Ops:
  6.6 0.9 slice_bitcast_fusion.8
  7.5 0.8 slice_bitcast_fusion.9
  8.3 0.7 slice_bitcast_fusion.12
  9.0 0.8 fusion.103
  9.9 0.6 pad_maximum_fusion.3
  10.7 0.7 pad_maximum_fusion.4
  11.4 1.0 fusion.85
  12.3 2.2 add_convert_fusion
  14.5 3.5 %all-to-all-start = ((bf16[4,6,24,512]{3,1,0,2:T(8,128)(2,1)}), bf16[4,6,24,512]{3,1,0,2:T(8,128)(2,1)S(1)}, u32[]{:S(2)}, u32[]{:S(2)}) async-start(bf16[4,6,24,512]{3,1,0,2:T(8,128)(2,1)} %add_convert_fusion), calls=%async_computation | async-start | bytes 1572864 | tf_op jit(solution)/shard_map/all_to_all | solution.py:196
  18.7 11.0 %all-to-all-done = bf16[4,6,24,512]{3,1,0,2:T(8,128)(2,1)S(1)} async-done(((bf16[4,6,24,512]{3,1,0,2:T(8,128)(2,1)}), bf16[4,6,24,512]{3,1,0,2:T(8,128)(2,1)S(1)}, u32[]{:S(2)}, u32[]{:S(2)}) %all-to-all-start) | async-done | bytes 589856 | tf_op jit(solution)/shard_map/all_to_all | solution.py:196
  30.3 0.8 convolution_convert_fusion.2
  31.1 1.0 copy-done.8
  32.6 1.6 reshape.291
  34.2 1.1 slice_convert_fusion
  35.4 1.4 reshape.294
  37.1 1.4 subtract_exponential_fusion.2
  38.6 3.0 %multiply_reduce_fusion.2 = f32[6,12,4,512]{3,1,2,0:T(8,128)S(1)} fusion(f32[8,6,12,512]{3,2,1,0:T(8,128)S(1)} %reshape.294, f32[8,6,12,4,16]{4,3,2,1,0:T(4,128)S(1)} %bitcast.111, s32[512]{0:T(512)S(1)} %add_select_fusion), kind=kOutput, calls=%fused_computation.4 | convolution fusion | flops 228712448 | bytes 1918976 | tf_op jit(solution)/shard_map/dot_general | solution.py:76
  41.6 0.5 fusion.38
  42.1 0.6 copy-done.15
  42.6 0.4 fusion.37
  43.1 0.6 fusion.98
  43.7 1.2 reshape.295
  44.9 0.5 multiply_reduce_fusion.7
  45.4 0.4 multiply_convert_fusion.3
  46.0 43.5 %all-gather.5.cloned.1.call-done = bf16[3145728]{0:T(1024)(128)(2,1)} async-done(((bf16[49152]{0:T(1024)(128)(2,1)}), bf16[3145728]{0:T(1024)(128)(2,1)}) %all-gather.5.cloned.1.call-update) | async-done | bytes 6291472 | tf_op jit(solution)/shard_map/all_gather | solution.py:24
  89.5 8.9 %reshape.301 = bf16[64,49152]{1,0:T(8,128)(2,1)} reshape(bf16[3145728]{0:T(1024)(128)(2,1)} %all-gather.5.cloned.1.call-done) | data formatting | bytes 12582912 | tf_op jit(solution)/shard_map/all_gather | solution.py:24
  98.4 1.4 slice-done.2
  99.8 1.6 reshape_reshape.32
  101.4 2.1 convolution_convert_fusion.1
  103.5 0.9 copy-done.10
  104.5 1.0 reshape_reshape.33
  105.5 3.9 %fusion.100 = (bf16[64,16384]{1,0:T(8,128)(2,1)S(1)}, bf16[64,16384]{1,0:T(8,128)(2,1)}) fusion(bf16[64,49152]{1,0:T(8,128)(2,1)} %reshape.301), kind=kLoop, calls=%fused_computation.165 | loop fusion | bytes 8388608 | tf_op jit(solution)/shard_map/slice | solution.py:26
  109.4 4.2 %reshape_reshape.35 = bf16[2048,512]{1,0:T(8,128)(2,1)} reshape(bf16[64,16384]{1,0:T(8,128)(2,1)} %get-tuple-element.35) | data formatting | bytes 4194304 | tf_op jit(solution)/shard_map/reshape;reshape | solution.py:19
  113.6 2.4 %reshape_reshape.34 = bf16[512,2048]{1,0:T(8,128)(2,1)} reshape(bf16[64,16384]{1,0:T(8,128)(2,1)S(1)} %get-tuple-element.34) | data formatting | bytes 4194304 | tf_op jit(solution)/shard_map/reshape;reshape | solution.py:19
  116.0 2.4 %fusion.4 = f32[2,16,144,144]{2,3,1,0:T(8,128)S(1)} fusion(bf16[16,512]{1,0:T(8,128)(2,1)S(1)} %get-tuple-element.65, bf16[2,144,512]{2,1,0:T(8,128)(2,1)S(1)} %slice.181, bf16[2,144,1536]{2,1,0:T(8,128)(2,1)} %bitcast.126), kind=kOutput, calls=%fused_computation.12 | convolution fusion | flops 681836544 | bytes 3260416 | tf_op jit(solution)/shard_map/while/body/eval_jaxpr/nhad,nbd->nhab/dot_general | solution.py:119
  118.4 4.7 %fusion.107 = (f32[2,16,144]{2,1,0:T(8,128)S(1)}, f32[2,16,144,144]{2,3,1,0:T(8,128)S(1)}) fusion(f32[2,16,144,144]{2,3,1,0:T(8,128)S(1)} %fusion.4), kind=kOutput, calls=%fused_computation.172 | output fusion | flops 2654351 | bytes 5326848 | tf_op jit(solution)/shard_map/while/body/eval_jaxpr/sub | solution.py:126
  123.1 2.8 %multiply_reduce_fusion.1 = bf16[2,144,512]{2,1,0:T(8,128)(2,1)S(1)} fusion(f32[16,512]{1,0:T(8,128)S(1)} %get-tuple-element.64, f32[2,16,144,144]{2,3,1,0:T(8,128)S(1)} %get-tuple-element.69, f32[2,16,144]{2,1,0:T(8,128)S(1)} %get-tuple-element.68, bf16[2,144,1536]{2,1,0:T(8,128)(2,1)} %bitcast.127), kind=kOutput, calls=%fused_computation.3 | convolution fusion | flops 685375488 | bytes 3295232 | tf_op jit(solution)/shard_map/while/body/eval_jaxpr/nhab,nbd->nhad/dot_general | solution.py:128
  125.9 0.4 fusion.108
  126.6 4.0 %fusion.39 = bf16[288,512]{1,0:T(8,128)(2,1)S(1)} fusion(f32[288,512]{1,0:T(8,128)S(1)} %get-tuple-element.71, bf16[2048,512]{1,0:T(8,128)(2,1)} %reshape_reshape.35, bf16[512,2048]{1,0:T(8,128)(2,1)} %reshape_reshape.34, f32[512]{0:T(512)S(1)} %bitcast.138, f32[288]{0:T(512)S(1)} %add_rsqrt_fusion.3, f32[288]{0:T(512)S(1)} %broadcast_multiply_fusion.4), kind=kOutput, calls=%fused_computation.58 | convolution fusion | flops 1214152704 | bytes 5083392 | tf_op jit(solution)/shard_map/dot_general | solution.py:140
  131.3 0.3 fusion.73
  131.6 4.7 %collective-permute-start = (bf16[3,12,4,512]{3,2,1,0:T(4,128)(2,1)S(1)}, bf16[3,12,4,512]{3,2,1,0:T(4,128)(2,1)S(1)}, u32[]{:S(2)}, u32[]{:S(2)}) collective-permute-start(bf16[3,12,4,512]{3,2,1,0:T(4,128)(2,1)S(1)} %get-tuple-element.37), channel_id=1, source_target_pairs={{1,0},{2,1},{3,2},{4,3},{5,4},{6,5},{7,6},{8,7},{9,8},{10,9},{11,1... | collective-permute-start | bytes 442376 | tf_op jit(solution)/shard_map/ppermute | solution.py:35
  136.4 31.5 %all-gather.7.cloned.1.call-done = bf16[3145728]{0:T(1024)(128)(2,1)} async-done(((bf16[49152]{0:T(1024)(128)(2,1)}), bf16[3145728]{0:T(1024)(128)(2,1)}) %all-gather.7.cloned.1.call-update) | async-done | bytes 6291472 | tf_op jit(solution)/shard_map/all_gather | solution.py:24
  167.9 8.8 %reshape.302 = bf16[64,49152]{1,0:T(8,128)(2,1)} reshape(bf16[3145728]{0:T(1024)(128)(2,1)} %all-gather.7.cloned.1.call-done) | data formatting | bytes 12582912 | tf_op jit(solution)/shard_map/all_gather | solution.py:24
  177.0 0.6 collective-permute-start.1
  177.6 4.5 %fusion.99 = (bf16[64,16384]{1,0:T(8,128)(2,1)}, bf16[64,16384]{1,0:T(8,128)(2,1)}) fusion(bf16[64,49152]{1,0:T(8,128)(2,1)} %reshape.302), kind=kLoop, calls=%fused_computation.164 | loop fusion | bytes 8388608 | tf_op jit(solution)/shard_map/slice | solution.py:26
  182.1 1.4 slice-done
  183.5 1.6 reshape_reshape.37
  185.2 1.1 reshape_reshape.38
  186.2 4.4 %reshape_reshape.40 = bf16[2048,512]{1,0:T(8,128)(2,1)} reshape(bf16[64,16384]{1,0:T(8,128)(2,1)} %get-tuple-element.33) | data formatting | bytes 4194304 | tf_op jit(solution)/shard_map/reshape;reshape | solution.py:19
  190.6 2.3 %reshape_reshape.39 = bf16[512,2048]{1,0:T(8,128)(2,1)} reshape(bf16[64,16384]{1,0:T(8,128)(2,1)S(1)} %copy-done.2) | data formatting | bytes 4194304 | tf_op jit(solution)/shard_map/reshape;reshape | solution.py:19
  193.1 0.5 reshape.300
  194.1 0.4 reshape.296
  194.9 0.5 multiply_reduce_fusion.5
  195.8 0.4 multiply_convert_fusion.1
  196.5 0.6 convolution_convert_fusion
  197.2 1.4 fusion.2
  198.6 1.5 fusion.109
  200.1 1.7 multiply_reduce_fusion
  201.9 0.4 fusion.110
  202.6 4.0 %fusion.40 = bf16[288,512]{1,0:T(8,128)(2,1)S(1)} fusion(f32[288,512]{1,0:T(8,128)S(1)} %get-tuple-element.75, bf16[2048,512]{1,0:T(8,128)(2,1)} %reshape_reshape.40, bf16[512,2048]{1,0:T(8,128)(2,1)} %reshape_reshape.39, f32[512]{0:T(512)S(1)} %bitcast.137, f32[288]{0:T(512)S(1)} %add_rsqrt_fusion.2, f32[288]{0:T(512)S(1)} %broadcast_multiply_fusion.3), kind=kOutput, calls=%fused_computation.59 | convolution fusion | flops 1214152704 | bytes 5083392 | tf_op jit(solution)/shard_map/dot_general | solution.py:140
  207.4 10.1 %collective-permute-done.2 = bf16[3,12,4,512]{3,2,1,0:T(4,128)(2,1)S(1)} collective-permute-done((bf16[3,12,4,512]{3,2,1,0:T(4,128)(2,1)S(1)}, bf16[3,12,4,512]{3,2,1,0:T(4,128)(2,1)S(1)}, u32[]{:S(2)}, u32[]{:S(2)}) %collective-permute-start.2) | collective-permute-done | bytes 147488 | tf_op jit(solution)/shard_map/ppermute | solution.py:35
  217.7 1.5 collective-permute-start.3
  219.3 3.7 %collective-permute-done.3 = bf16[6,6,4,512]{3,2,1,0:T(4,128)(2,1)S(1)} collective-permute-done((bf16[6,6,4,512]{3,2,1,0:T(4,128)(2,1)S(1)}, bf16[6,6,4,512]{3,2,1,0:T(4,128)(2,1)S(1)}, u32[]{:S(2)}, u32[]{:S(2)}) %collective-permute-start.3) | collective-permute-done | bytes 147488 | tf_op jit(solution)/shard_map/ppermute | solution.py:39
  223.2 1.0 fusion.57
  (108 shorter events, 7.0 us)
Async XLA Ops:
  6.5 23.7 %copy-start = (bf16[512,1024]{1,0:T(8,128)(2,1)S(1)}, bf16[512,1024]{1,0:T(8,128)(2,1)}, u32[]{:S(2)}) copy-start(bf16[512,1024]{1,0:T(8,128)(2,1)} %param.19) | copy-start | bytes 3145732
  6.5 11.6 %copy-start.13 = (f32[2,512]{1,0:T(2,128)S(1)}, f32[2,512]{1,0:T(2,128)}, u32[]{:S(2)}) copy-start(f32[2,512]{1,0:T(2,128)} %param.22) | copy-start | bytes 12292
  6.5 11.6 %copy-start.12 = (bf16[4,512]{1,0:T(4,128)(2,1)S(1)}, bf16[4,512]{1,0:T(4,128)(2,1)}, u32[]{:S(2)}) copy-start(bf16[4,512]{1,0:T(4,128)(2,1)} %param.17) | copy-start | bytes 12292
  6.5 11.6 %copy-start.7 = (bf16[512,512]{1,0:T(8,128)(2,1)S(1)}, bf16[512,512]{1,0:T(8,128)(2,1)}, u32[]{:S(2)}) copy-start(bf16[512,512]{1,0:T(8,128)(2,1)} %param.18) | copy-start | bytes 1572868
  6.5 83.0 %all-gather.5.cloned.1.call-start = ((), (), s32[]{:S(2)}) async-start(), calls=%async_computation.1 | async-start | bytes 6389760 | tf_op jit(solution)/shard_map/all_gather | solution.py:24
  8.3 10.0 %copy-start.14 = (f32[2,512]{1,0:T(2,128)S(1)}, f32[2,512]{1,0:T(2,128)}, u32[]{:S(2)}) copy-start(f32[2,512]{1,0:T(2,128)} %param.23) | copy-start | bytes 12292
  8.3 10.1 %copy-start.11 = (s32[6,12,4]{1,2,0:T(4,128)S(1)}, s32[6,12,4]{1,2,0:T(4,128)}, u32[]{:S(2)}) copy-start(s32[6,12,4]{1,2,0:T(4,128)} %param.21) | copy-start | bytes 3460
  10.5 157.4 %all-gather.7.cloned.1.call-start = ((), (), s32[]{:S(2)}) async-start(), calls=%async_computation.2 | async-start | bytes 6389760 | tf_op jit(solution)/shard_map/all_gather | solution.py:24
  14.5 15.1 %all-to-all-start = ((bf16[4,6,24,512]{3,1,0,2:T(8,128)(2,1)}), bf16[4,6,24,512]{3,1,0,2:T(8,128)(2,1)S(1)}, u32[]{:S(2)}, u32[]{:S(2)}) async-start(bf16[4,6,24,512]{3,1,0,2:T(8,128)(2,1)} %add_convert_fusion), calls=%async_computation | async-start | bytes 1572864 | tf_op jit(solution)/shard_map/all_to_all | solution.py:196
  31.1 1.0 copy-start.8
  32.4 1.8 copy-start.9
  41.6 1.0 copy-start.15
  98.4 1.4 slice-start.2
  101.4 3.1 %slice-start.3 = ((bf16[64,49152]{1,0:T(8,128)(2,1)}), bf16[64,4096]{1,0:T(8,128)(2,1)S(1)}, s32[]{:S(2)}) async-start(bf16[64,49152]{1,0:T(8,128)(2,1)} %reshape.301), calls=%async_computation.6 | async-start | bytes 1048576 | tf_op jit(solution)/shard_map/slice | solution.py:26
  103.5 0.9 copy-start.10
  123.1 2.8 %copy-start.3 = (f32[288,512]{1,0:T(8,128)S(1)}, f32[288,512]{1,0:T(8,128)}, u32[]{:S(2)}) copy-start(f32[288,512]{1,0:T(8,128)} %reshape.295) | copy-start | bytes 1769476
  123.1 2.8 %copy-start.5 = (bf16[512,512]{1,0:T(8,128)(2,1)S(1)}, bf16[512,512]{1,0:T(8,128)(2,1)}, u32[]{:S(2)}) copy-start(bf16[512,512]{1,0:T(8,128)(2,1)} %reshape_reshape.33) | copy-start | bytes 1572868
  131.6 45.1 %collective-permute-start = (bf16[3,12,4,512]{3,2,1,0:T(4,128)(2,1)S(1)}, bf16[3,12,4,512]{3,2,1,0:T(4,128)(2,1)S(1)}, u32[]{:S(2)}, u32[]{:S(2)}) collective-permute-start(bf16[3,12,4,512]{3,2,1,0:T(4,128)(2,1)S(1)} %get-tuple-element.37), channel_id=1, source_target_pairs={{1,0},{2,1},{3,2},{4,3},{5,4},{6,5},{7,6},{8,7},{9,8},{10,9},{11,1... | collective-permute-start | bytes 442376 | tf_op jit(solution)/shard_map/ppermute | solution.py:35
  177.0 16.0 %collective-permute-start.1 = (bf16[6,6,4,512]{3,2,1,0:T(4,128)(2,1)S(1)}, bf16[6,6,4,512]{3,2,1,0:T(4,128)(2,1)S(1)}, u32[]{:S(2)}, u32[]{:S(2)}) collective-permute-start(bf16[6,6,4,512]{3,2,1,0:T(4,128)(2,1)S(1)} %get-tuple-element.51), channel_id=1, source_target_pairs={{0,64},{64,0},{1,65},{65,1},{2,66},{66,2},{3,67},{67,3},{4,68},{68... | collective-permute-start | bytes 442376 | tf_op jit(solution)/shard_map/ppermute | solution.py:39
  182.1 1.4 slice-start
  182.1 3.0 %slice-start.1 = ((bf16[64,49152]{1,0:T(8,128)(2,1)}), bf16[64,4096]{1,0:T(8,128)(2,1)S(1)}, s32[]{:S(2)}) async-start(bf16[64,49152]{1,0:T(8,128)(2,1)} %reshape.302), calls=%async_computation.4 | async-start | bytes 1048576 | tf_op jit(solution)/shard_map/slice | solution.py:26
  186.2 4.4 %copy-start.2 = (bf16[64,16384]{1,0:T(8,128)(2,1)S(1)}, bf16[64,16384]{1,0:T(8,128)(2,1)}, u32[]{:S(2)}) copy-start(bf16[64,16384]{1,0:T(8,128)(2,1)} %get-tuple-element.32) | copy-start | bytes 6291460
  194.5 2.0 copy-start.6
  200.1 1.7 copy-start.4
  202.6 21.7 %copy-start.1 = (bf16[512,1024]{1,0:T(8,128)(2,1)S(1)}, bf16[512,1024]{1,0:T(8,128)(2,1)}, u32[]{:S(2)}) copy-start(bf16[512,1024]{1,0:T(8,128)(2,1)} %param.19) | copy-start | bytes 3145732
  207.1 10.4 %collective-permute-start.2 = (bf16[3,12,4,512]{3,2,1,0:T(4,128)(2,1)S(1)}, bf16[3,12,4,512]{3,2,1,0:T(4,128)(2,1)S(1)}, u32[]{:S(2)}, u32[]{:S(2)}) collective-permute-start(bf16[3,12,4,512]{3,2,1,0:T(4,128)(2,1)S(1)} %slice.171), channel_id=1, source_target_pairs={{63,0},{0,1},{1,2},{2,3},{3,4},{4,5},{5,6},{6,7},{7,8},{8,9},{9,10... | collective-permute-start | bytes 442376 | tf_op jit(solution)/shard_map/ppermute | solution.py:35
  217.7 5.2 %collective-permute-start.3 = (bf16[6,6,4,512]{3,2,1,0:T(4,128)(2,1)S(1)}, bf16[6,6,4,512]{3,2,1,0:T(4,128)(2,1)S(1)}, u32[]{:S(2)}, u32[]{:S(2)}) collective-permute-start(bf16[6,6,4,512]{3,2,1,0:T(4,128)(2,1)S(1)} %get-tuple-element.44), channel_id=1, source_target_pairs={{0,64},{64,0},{1,65},{65,1},{2,66},{66,2},{3,67},{67,3},{4,68},{68... | collective-permute-start | bytes 442376 | tf_op jit(solution)/shard_map/ppermute | solution.py:39
Sparse Core Ops, SparseCore 0:
  10.7 78.8 all-gather.4
  92.7 75.1 all-gather.6
where the time goes:
time: 232 us; the launch traced here: 231 us
  waiting for transfers between devices  99.8 us (43%)
  local copies, waits for them, and re-layouts  62.8 us (27%)
  matrix products  26 us (11%)
  other arithmetic  17.9 us (8%)
  between operations  14.1 us (6%)
  starting transfers between devices  10.5 us (5%)
    all_gather x2, waiting for transfers between devices, gather_packed(): lines, at, outs = (lax.all_gather(flat, axis), 0, [])  75 us
    another operation x8, local copies, waits for them, and re-layouts, joined_along(): pieces.reshape(*shape[:dim], shape[dim] * shape[dim + 1], *shape[dim + 2:])  18.6 us
    all_gather x2, local copies, waits for them, and re-layouts, gather_packed(): lines, at, outs = (lax.all_gather(flat, axis), 0, [])  17.7 us
    slice x10, local copies, waits for them, and re-layouts, gather_packed(): pieces = lines[:, at:at + a.size].reshape(-1, *a.shape)  11.2 us
    all_to_all x1, waiting for transfers between devices, local(): lax.all_to_all(summed, 'lev', split_axis=2, concat_axis=0, tiled=True)  11 us
    ppermute x2, waiting for transfers between devices, from_behind(): return lax.ppermute(block, axis, route)  10.1 us
    dot_general x2, matrix products, swin_block(): jnp.dot(hidden, w_down, preferred_element_type=jnp.float32)  7.98 us
    sub x2, other arithmetic, attend(): weight = jnp.exp(score - top)  6.22 us
  transfers between devices with their start and end apart: 7, of which 5 were waited for; matrix products, arithmetic and copies ran while one was open for 35% of the time, Pallas kernels for 0%

commit v1 on v0

v1 whole, which is shorter than its diff:
```python
import functools

import jax
import jax.numpy as jnp
import numpy as np
from jax import lax
from jax.experimental import pallas as pl
from jax.experimental.pallas import tpu as pltpu
from jax.sharding import PartitionSpec as P

HEADS = 16
HD = 32
Q_LAT = 4
D = 512
PAD = 80
EPS = 1e-05
BF = jnp.bfloat16
F32 = jnp.float32
EXP_SCALE = float(np.log2(np.e) / np.sqrt(HD))


MESH = pl.DeviceIdType.MESH
ORDERS = ((0, 1, 2), (1, 2, 0), (2, 0, 1))


class Place:
    def __init__(self):
        self.lev = lax.axis_index("lev")
        lat = lax.axis_index("lat")
        self.lat = lat
        self.core = lax.rem(lat, 2)
        xh = lax.rem(lat // 2, 2)
        self.pos = (xh * 2 + self.lev, lat // 16, lax.rem(lat // 4, 4))

    def device(self, axis=None, step=0, core=None):
        x, y, z = [lax.rem(p + step, 4) if a == axis else p for a, p in enumerate(self.pos)]
        c = self.core if core is None else core
        return (lax.rem(x, 2), ((y * 4 + z) * 2 + x // 2) * 2 + c)


def region(where, core):
    x, y, z = where
    full = slice(None)
    if x is None:
        xl, xh = full, full
    elif isinstance(x, tuple):
        xl, xh = x[1], full
    else:
        xl, xh = lax.rem(x, 2), x // 2

    def line(v):
        if v is None:
            return full
        if isinstance(v, tuple):
            return pl.ds(2 * v[1], 2)
        return v

    return (xl, line(y), line(z), xh, core)


class Gather:
    def __init__(self, place, bufs, send, recv):
        self.place, self.bufs, self.send, self.recv = place, bufs, send, recv

    def copy(self, b, p, slot, where, core, device):
        at = self.bufs[p].at[(b,) + region(where, core)]
        return pltpu.make_async_remote_copy(
            src_ref=at,
            dst_ref=at,
            send_sem=self.send.at[b, p, slot],
            recv_sem=self.recv.at[b, p, slot],
            device_id=device,
            device_id_type=MESH,
        )

    def where(self, p, phase, step, half=None):
        order = ORDERS[p]
        place = [None, None, None]
        for k, axis in enumerate(order):
            if k == phase:
                place[axis] = lax.rem(self.place.pos[axis] + step + 4, 4)
            elif k > phase:
                place[axis] = self.place.pos[axis]
            elif k == 0 and half is not None:
                place[axis] = ("half", half)
        return place

    def going(self, b, p, slot):
        pl_ = self.place
        c = pl_.core
        if slot < 3:
            return self.copy(b, p, slot, self.where(p, 0, 0), c, pl_.device(ORDERS[p][0], (1, 3, 2)[slot]))
        if slot < 11:
            phase, k = 1 + (slot - 3) // 4, (slot - 3) % 4
            step, half, to = ((0, None, 1), (0, None, 3), (-1, 0, 1), (1, 1, 3))[k]
            return self.copy(b, p, slot, self.where(p, phase, step, half), c, pl_.device(ORDERS[p][phase], to))
        step = (0, -1, 1, 2)[slot - 11]
        return self.copy(b, p, slot, self.where(p, 2, step), c, pl_.device(core=1 - c))

    def coming(self, b, p, slot):
        pl_ = self.place
        c = pl_.core
        if slot < 3:
            step = (-1, 1, 2)[slot]
            return self.copy(b, p, slot, self.where(p, 0, step), c, pl_.device(ORDERS[p][0], (3, 1, 2)[slot]))
        if slot < 11:
            phase, k = 1 + (slot - 3) // 4, (slot - 3) % 4
            step, half, to = ((-1, None, 3), (1, None, 1), (2, 0, 3), (2, 1, 1))[k]
            return self.copy(b, p, slot, self.where(p, phase, step, half), c, pl_.device(ORDERS[p][phase], to))
        step = (0, -1, 1, 2)[slot - 11]
        return self.copy(b, p, slot, self.where(p, 2, step), 1 - c, pl_.device(core=1 - c))

    STAGES = (
        ((), (0, 1, 2)),
        ((0, 1, 2), (3, 4)),
        ((3, 4), (5, 6)),
        ((5, 6), (7, 8, 11)),
        ((7, 8), (9, 10, 12, 13)),
        ((9, 10), (14,)),
    )

    def stage(self, b, k, parts=(0, 1, 2)):
        waits, sends = self.STAGES[k]
        for p in parts:
            for slot in waits:
                self.coming(b, p, slot).wait_recv()
            for slot in sends:
                self.going(b, p, slot).start()

    def finish(self, b, parts=(0, 1, 2)):
        for p in parts:
            for slot in (11, 12, 13, 14):
                self.coming(b, p, slot).wait_recv()

    def drain(self, b, parts=(0, 1, 2)):
        for p in parts:
            for slot in range(15):
                self.going(b, p, slot).wait_send()


def greet(place, more):
    barrier = pltpu.get_barrier_semaphore()
    peers = [place.device(axis, step) for axis in range(3) for step in (1, 2, 3)]
    peers.append(place.device(core=1 - place.core))
    peers += more
    for peer in peers:
        pl.semaphore_signal(barrier, inc=1, device_id=peer, device_id_type=MESH)
    return barrier, len(peers)


def dot(a, b, dims=((1,), (0,))):
    return lax.dot_general(a, b, (dims, ((), ())), preferred_element_type=F32)


def layer_norm(flat, gain):
    mean = jnp.mean(flat, -1, keepdims=True)
    centred = flat - mean
    var = jnp.mean(centred * centred, -1, keepdims=True)
    return (centred * lax.rsqrt(var + EPS) * gain).astype(BF)


def gelu(x):
    inner = x * (0.7978845608028654 + 0.035677408136300125 * x * x)
    half = 0.5 * x
    return half + half * jnp.tanh(inner)


def one_hot(rows, columns, pairs):
    out = np.zeros((rows, columns), np.float32)
    for i, j in pairs:
        out[i, j] = 1.0
    return out


def cells():
    for k in range(4):
        for r in range(6):
            for c in range(12):
                yield k, r, c


def quarter_row(k, r, c):
    return ((r // 3) * 2 + c // 6) * PAD + k * 18 + (r % 3) * 6 + c % 6


def row_orders():
    halves = np.stack(
        [
            one_hot(
                2 * PAD,
                144,
                [
                    (side * PAD + r * 12 + c, r * 24 + c + 12 * (lev ^ side))
                    for side in range(2)
                    for r in range(6)
                    for c in range(12)
                ],
            )
            for lev in range(2)
        ]
    )
    cut = one_hot(4 * PAD, 288, [(quarter_row(k, r, c), k * 72 + r * 12 + c) for k, r, c in cells()])
    rolled = one_hot(
        288, 4 * PAD, [(k * 72 + r * 12 + c, quarter_row((k + 1) % 4, r, c)) for k, r, c in cells()]
    )
    back = one_hot(
        288, 4 * PAD, [(r * 48 + c * 4 + (k + 1) % 4, quarter_row(k, r, c)) for k, r, c in cells()]
    )
    return [a.astype(BF) for a in (halves, cut, rolled, back)]


def head_spread():
    rows = np.arange(Q_LAT * HEADS)
    return (np.arange(D)[None, :] // HD == rows[:, None] % HEADS).astype(BF)


def pick_head(shape, j):
    lane = lax.broadcasted_iota(jnp.int32, shape, 1)
    return (lane >= j * HD) & (lane < (j + 1) * HD)


def attention(q, k, v, mask):
    parts = []
    for g in range(4):
        lanes = slice(g * 128, (g + 1) * 128)
        kg, vg, qg = k[:, lanes], v[:, lanes], q[:, lanes]
        heads = [pick_head((144, 128), j) for j in range(4)]
        qs = jnp.concatenate([jnp.where(h, qg, jnp.zeros_like(qg)) for h in heads], 0)
        score = dot(kg, qs, ((1,), (1,)))
        if mask is not None:
            score = jnp.where(mask, score, -1e30)
        top = jnp.max(score, 0, keepdims=True)
        weight = jnp.exp2((score - top) * EXP_SCALE)
        weight = (weight * (1.0 / jnp.sum(weight, 0, keepdims=True))).astype(BF)
        out = dot(weight, vg, ((0,), (0,)))
        ctx = jnp.zeros((144, 128), F32)
        for j, h in enumerate(heads):
            ctx = jnp.where(h, out[j * 144 : (j + 1) * 144], ctx)
        parts.append(ctx.astype(BF))
    return jnp.concatenate(parts, 1)


class Block:
    def __init__(self, b, bufs, gain_one, gain_two):
        self.b, self.bufs = b, bufs
        self.gain_one = gain_one[b : b + 1, :]
        self.gain_two = gain_two[b : b + 1, :]

    def attend(self, x, regions=None):
        b, wa = self.b, self.bufs[0]
        n1 = layer_norm(x, self.gain_one)
        qk = dot(n1, wa[b, 0].reshape(D, 1024)).astype(BF)
        wv = wa[b, 1, :, :, :, :, :, 0:512].reshape(D, D)
        v = dot(n1, wv).astype(BF)
        out = []
        for w in range(2):
            rows = slice(w * 144, (w + 1) * 144)
            mask = None
            if regions is not None:
                kinds = lax.broadcasted_iota(jnp.int32, (8, 144), 0)
                ids = jnp.broadcast_to(regions[w : w + 1, :], (8, 144))
                hot = (kinds == ids).astype(F32).astype(BF)
                same = dot(hot, hot, ((0,), (0,)))
                mask = jnp.concatenate([same] * 4, 1) > 0.5
            out.append(attention(qk[rows, 0:D], qk[rows, D : 2 * D], v[rows], mask))
        return jnp.concatenate(out, 0)

    def mix(self, x, context):
        wp = self.bufs[0][self.b, 1, :, :, :, :, :, 512:1024].reshape(D, D)
        return (x + dot(context, wp)).astype(BF).astype(F32)

    def feed(self, mixed):
        b = self.b
        n2 = layer_norm(mixed, self.gain_two)
        sums = [0.0, 0.0]
        for h in range(2):
            hidden = gelu(dot(n2, self.bufs[1][b, h].reshape(D, 1024))).astype(BF)
            for side in range(2):
                wd = self.bufs[2][b, side, 2 * h : 2 * h + 2].reshape(1024, 256)
                sums[side] = sums[side] + dot(hidden, wd)
        return (mixed + jnp.concatenate(sums, 1)).astype(BF)


def moved(send_buf, recv_buf, sems, slot, peer, quarter):
    return pltpu.make_async_remote_copy(
        src_ref=send_buf.at[quarter],
        dst_ref=recv_buf.at[slot],
        send_sem=sems[0].at[slot],
        recv_sem=sems[1].at[slot],
        device_id=peer,
        device_id_type=MESH,
    )


def kernel(
    level_ids,
    tokens,
    level_table,
    latent_query,
    w_query,
    w_kv,
    w_attn_out,
    regions,
    gain_one,
    gain_two,
    w_qkv,
    w_proj,
    w_up,
    w_down,
    spread,
    halves,
    cut,
    roll_rows,
    back_rows,
    out,
    ba,
    bb,
    bc,
    tok_own,
    tok_send,
    tok_recv,
    hs,
    hr,
    hs2,
    hr2,
    send,
    recv,
    tok_sem,
    hsem,
    hrsem,
    h2sem,
    h2rsem,
):
    place = Place()
    lev, lat = place.lev, place.lat
    partner = (1 - lev, lat)
    ahead, behind = lax.rem(lat + 1, 64), lax.rem(lat + 63, 64)
    barrier, count = greet(place, [(lev, ahead), (lev, behind), (1 - lev, ahead), (1 - lev, behind)])
    bufs = (ba, bb, bc)
    g = Gather(place, bufs, send, recv)
    first = lev == 0
    for blk in range(2):
        at = (blk,) + region(place.pos, place.core)
        qkv = w_qkv[blk]
        proj = w_proj[blk]
        ba[at] = jnp.where(first, qkv[:, 0:1024], jnp.concatenate([qkv[:, 1024:1536], proj], 1))
        up = w_up[blk]
        bb[at] = jnp.where(first, up[:, 0:1024], up[:, 1024:2048])
        down = w_down[blk]
        bc[at] = jnp.where(first, down[:, 0:256], down[:, 256:512])
    select = halves[lev]
    for slot in range(4):
        row = level_table[pl.ds(level_ids[slot], 1), :]
        summed = (tokens[slot].astype(F32).reshape(144, D) + row).astype(BF)
        both = dot(select, summed).astype(BF)
        tok_own[slot] = both[0:PAD]
        tok_send[slot] = both[PAD : 2 * PAD]
    pl.semaphore_wait(barrier, count)

    g.stage(0, 0)
    tok = pltpu.make_async_remote_copy(
        src_ref=tok_send,
        dst_ref=tok_recv,
        send_sem=tok_sem.at[0],
        recv_sem=tok_sem.at[1],
        device_id=partner,
        device_id_type=MESH,
    )
    tok.start()
    g.stage(1, 0)

    queries = dot(latent_query[...], w_query[...]).astype(BF).astype(F32)
    wide_q = jnp.concatenate(
        [jnp.broadcast_to(queries[q : q + 1], (HEADS, D)) for q in range(Q_LAT)], 0
    )
    query_block = (wide_q * spread[...].astype(F32)).astype(BF)

    def keys_values(ref):
        kv = dot(ref[...].astype(F32).reshape(4 * PAD, D).astype(BF), w_kv[...]).astype(BF)
        score = dot(kv[:, 0:D], query_block, ((1,), (1,)))
        return score.reshape(4, PAD, Q_LAT * HEADS), kv[:, D : 2 * D].astype(F32).reshape(4, PAD, D)

    score_own, val_own = keys_values(tok_own)
    g.stage(0, 1)
    g.stage(1, 1)
    g.stage(0, 2)
    g.stage(1, 2)
    tok.wait_recv()
    score_par, val_par = keys_values(tok_recv)
    g.stage(0, 3)
    top = jnp.maximum(jnp.max(score_own, 0), jnp.max(score_par, 0))
    w_own = jnp.exp2((score_own - top) * EXP_SCALE)
    w_par = jnp.exp2((score_par - top) * EXP_SCALE)
    inverse = 1.0 / (jnp.sum(w_own, 0) + jnp.sum(w_par, 0))
    w_own = (w_own * inverse).reshape(4 * PAD, Q_LAT * HEADS).astype(BF)
    w_par = (w_par * inverse).reshape(4 * PAD, Q_LAT * HEADS).astype(BF)
    attended = []
    line = lax.broadcasted_iota(jnp.int32, (Q_LAT * HEADS, D), 0)
    for q in range(Q_LAT):
        mine = (line >= q * HEADS) & (line < (q + 1) * HEADS)
        owner = jnp.where(mine, spread[...], jnp.zeros((Q_LAT * HEADS, D), BF))
        total = jnp.sum(dot(w_own, owner).reshape(4, PAD, D) * val_own, 0)
        total = total + jnp.sum(dot(w_par, owner).reshape(4, PAD, D) * val_par, 0)
        attended.append(total[0:72])
    g.stage(0, 4)
    attended = jnp.concatenate(attended, 0).astype(BF)
    base = jnp.concatenate([jnp.broadcast_to(queries[q : q + 1], (72, D)) for q in range(Q_LAT)], 0)
    x = (dot(attended, w_attn_out[...]) + base).astype(BF).astype(F32)
    g.stage(1, 3)
    g.stage(0, 5)
    g.finish(0)

    block = Block(0, bufs, gain_one, gain_two)
    context = block.attend(x)
    g.stage(1, 4)
    mixed = block.mix(x, context)
    plain = block.feed(mixed)
    g.stage(1, 5)
    quarters = dot(cut[...], plain).astype(BF)
    for n in range(4):
        hs[n] = quarters[n * PAD : (n + 1) * PAD]
    sems = (hsem, hrsem)
    sent = [
        moved(hs, hr, sems, 0, partner, 2),
        moved(hs, hr, sems, 1, (lev, behind), 1),
        moved(hs, hr, sems, 2, (1 - lev, behind), 0),
    ]
    for copy in sent:
        copy.start()
    g.finish(1)
    for copy in sent:
        copy.wait_recv()
    tiles = jnp.concatenate([hs[3], hr[0], hr[1], hr[2]], 0)
    x = dot(roll_rows[...], tiles)

    block = Block(1, bufs, gain_one, gain_two)
    context = block.attend(x, regions)
    mixed = block.mix(x, context)
    shifted = block.feed(mixed)
    quarters = dot(cut[...], shifted).astype(BF)
    for n in range(4):
        hs2[n] = quarters[n * PAD : (n + 1) * PAD]
    sems = (h2sem, h2rsem)
    back = [
        moved(hs2, hr2, sems, 0, partner, 1),
        moved(hs2, hr2, sems, 1, (lev, ahead), 2),
        moved(hs2, hr2, sems, 2, (1 - lev, ahead), 3),
    ]
    for copy in back:
        copy.start()
    for copy in back:
        copy.wait_recv()
    tiles = jnp.concatenate([hr2[2], hr2[1], hr2[0], hs2[0]], 0)
    out[...] = dot(back_rows[...], tiles).astype(BF)

    tok.wait_send()
    g.drain(0)
    g.drain(1)
    for copy in sent + back:
        copy.wait_send()


def local(
    tokens,
    level_ids,
    level_table,
    latent_query,
    w_query,
    w_kv,
    w_attn_out,
    regions,
    gain_one,
    gain_two,
    w_qkv,
    w_proj,
    w_up,
    w_down,
):
    labels = jnp.transpose(regions, (2, 0, 1)).reshape(2, 144)
    vmem = pl.BlockSpec(memory_space=pltpu.VMEM)
    consts = [jnp.asarray(head_spread())] + [jnp.asarray(a) for a in row_orders()]
    buf = pltpu.VMEM
    dma = pltpu.SemaphoreType.DMA
    flat = pl.pallas_call(
        kernel,
        out_shape=jax.ShapeDtypeStruct((288, D), BF),
        in_specs=[pl.BlockSpec(memory_space=pltpu.SMEM)] + [vmem] * 18,
        out_specs=vmem,
        scratch_shapes=[
            buf((2, 2, 4, 4, 2, 2, 8, 1024), BF),
            buf((2, 2, 4, 4, 2, 2, 8, 1024), BF),
            buf((2, 2, 4, 4, 2, 2, 32, 256), BF),
            buf((4, PAD, D), BF),
            buf((4, PAD, D), BF),
            buf((4, PAD, D), BF),
            buf((4, PAD, D), BF),
            buf((3, PAD, D), BF),
            buf((4, PAD, D), BF),
            buf((3, PAD, D), BF),
            dma((2, 3, 15)),
            dma((2, 3, 15)),
            dma((2,)),
            dma((3,)),
            dma((3,)),
            dma((3,)),
            dma((3,)),
        ],
        compiler_params=pltpu.CompilerParams(
            collective_id=0, has_side_effects=True, vmem_limit_bytes=56 << 20
        ),
        name="encode_and_blocks",
    )(
        level_ids,
        tokens,
        level_table,
        latent_query,
        w_query,
        w_kv,
        w_attn_out,
        labels,
        gain_one,
        gain_two,
        w_qkv,
        w_proj,
        w_up,
        w_down,
        *consts,
    )
    return flat.reshape(6, 12, Q_LAT, D)


def solution(mesh):
    in_specs = (
        P("lev", "lat", None, None),
        P("lev"),
        P(),
        P(),
        P(),
        P(),
        P(),
        P("lat", "lev", None),
        P(),
        P(),
        P(None, "lat", None),
        P(None, "lat", None),
        P(None, "lat", None),
        P(None, "lat", None),
    )
    out_specs = P("lat", "lev", None, None)
    return jax.shard_map(local, mesh=mesh, in_specs=in_specs, out_specs=out_specs, check_vma=False)
```

time: 232 us -> 74 us (0.32)
  waiting for transfers between devices: 99.8 us -> 0 us
  Pallas kernels: 0 us -> 70.6 us
  local copies, waits for them, and re-layouts: 62.8 us -> 3.12 us
  matrix products: 26 us -> 0 us
  other arithmetic: 17.9 us -> 0 us
  between operations: 14.1 us -> 0.01 us
  starting transfers between devices: 10.5 us -> 0 us
    all_gather x2 -> x0, waiting for transfers between devices: 75 us -> none  [gather_packed(): lines, at, outs = (lax.all_gather(flat, axis), 0, [])]
    pallas_call x0 -> x1, Pallas kernels: none -> 70.6 us  [local(): pl.pallas_call(kernel, out_shape=jax.ShapeDtypeStruct((288, D), BF), in_s...]
    dot_general x17 -> x0, matrix products: 26 us -> none  [the longest x2 7.98 us: swin_block(): jnp.dot(hidden, w_down, preferred_element_type=jnp.float32)]
    another operation x14 -> x0, local copies, waits for them, and re-layouts: 19.3 us -> none  [the longest x8 18.6 us: joined_along(): pieces.reshape(*shape[:dim], shape[dim] * shape[dim + 1], *shape[dim + 2:])]
    all_gather x2 -> x0, local copies, waits for them, and re-layouts: 17.7 us -> none  [gather_packed(): lines, at, outs = (lax.all_gather(flat, axis), 0, [])]
    ppermute x4 -> x0, waiting for transfers between devices: 13.8 us -> none  [the longest x2 10.1 us: from_behind(): return lax.ppermute(block, axis, route)]
    slice x23 -> x0, local copies, waits for them, and re-layouts: 13 us -> none  [the longest x10 11.2 us: gather_packed(): pieces = lines[:, at:at + a.size].reshape(-1, *a.shape)]
    all_to_all x1 -> x0, waiting for transfers between devices: 11 us -> none  [local(): lax.all_to_all(summed, 'lev', split_axis=2, concat_axis=0, tiled=True)]
  transfers between devices with their start and end apart: 7 -> 0, of which waited for: 5 -> 0; matrix products, arithmetic and copies ran while one was open for 35% -> 0% of each run, Pallas kernels for 0% -> 0%
where the time goes in v1:
time: 74 us; the launch traced here: 73.8 us
  Pallas kernels  70.6 us (95%)
  local copies, waits for them, and re-layouts  3.12 us (4%)
    pallas_call x1, Pallas kernels, local(): pl.pallas_call(kernel, out_shape=jax.ShapeDtypeStruct((288, D), BF), in_s...  70.6 us
    reshape x1, local copies, waits for them, and re-layouts, local(): return flat.reshape(6, 12, Q_LAT, D)  1.75 us

profile of v1, /device:TPU:0, one launch (start us, length us, event | category | flops | bytes accessed | tf_op | source)
XLA Modules:
  0.0 73.8 jit_solution(9382178645186853727)
XLA Ops:
  0.0 0.7 copy.21
  0.7 0.7 reshape.6.regions
  1.4 70.6 %encode_and_blocks.1 = bf16[288,512]{1,0:T(8,128)(2,1)} custom-call(s32[4]{0:T(128)} %level_ids.1, bf16[4,6,24,512]{3,2,1,0:T(8,128)(2,1)} %tokens.1, f32[13,512]{1,0:T(8,128)} %level_table.1, bf16[4,512]{1,0:T(4,128)(2,1)} %latent_query.1, bf16[512,512]{1,0:T(8,128)(2,1)} %w_query.1, bf16[512,1024]{1,0:T(8,128)(2,1)} %w_kv.1, bf16[512,512]{1,0:T(8,128)(2,1)} %w_attn_out.1, ...), custom_call_target="tpu_custom_call" | custom-call | tf_op jit(solution)/shard_map/encode_and_blocks/pallas_call | solution.py:484
  72.0 1.7 %reshape.7 = bf16[6,12,4,512]{3,2,1,0:T(4,128)(2,1)} reshape(bf16[288,512]{1,0:T(8,128)(2,1)} %encode_and_blocks.1) | data formatting | bytes 589824 | tf_op jit(solution)/shard_map/reshape | solution.py:529

commit v2 on v1

--- a/solution.py
+++ b/solution.py
@@ -44,7 +44,7 @@
     if x is None:
         xl, xh = full, full
     elif isinstance(x, tuple):
-        xl, xh = x[1], full
+        xl, xh = full, x[1]
     else:
         xl, xh = lax.rem(x, 2), x // 2
 
@@ -58,84 +58,95 @@
     return (xl, line(y), line(z), xh, core)
 
 
+SLOTS = 13
+EARLY = slice(0, 256)
+LATE = slice(256, 1024)
+STEPS = (1, 3, 2)
+
+
 class Gather:
     def __init__(self, place, bufs, send, recv):
         self.place, self.bufs, self.send, self.recv = place, bufs, send, recv
 
-    def copy(self, b, p, slot, where, core, device):
-        at = self.bufs[p].at[(b,) + region(where, core)]
+    def copy(self, p, slot, index, device):
+        at = self.bufs[p].at[index]
         return pltpu.make_async_remote_copy(
             src_ref=at,
             dst_ref=at,
-            send_sem=self.send.at[b, p, slot],
-            recv_sem=self.recv.at[b, p, slot],
+            send_sem=self.send.at[p, slot],
+            recv_sem=self.recv.at[p, slot],
             device_id=device,
             device_id_type=MESH,
         )
 
-    def where(self, p, phase, step, half=None):
+    def index(self, p, block, phase, step, core, columns, half=None):
         order = ORDERS[p]
-        place = [None, None, None]
+        where = [None, None, None]
         for k, axis in enumerate(order):
             if k == phase:
-                place[axis] = lax.rem(self.place.pos[axis] + step + 4, 4)
+                if isinstance(step, tuple):
+                    own = self.place.pos[axis] // 2
+                    where[axis] = ("pair", own if step[1] == 0 else 1 - own)
+                elif step is not None:
+                    where[axis] = lax.rem(self.place.pos[axis] + step, 4)
             elif k > phase:
-                place[axis] = self.place.pos[axis]
+                where[axis] = self.place.pos[axis]
             elif k == 0 and half is not None:
-                place[axis] = ("half", half)
-        return place
-
-    def going(self, b, p, slot):
-        pl_ = self.place
-        c = pl_.core
-        if slot < 3:
-            return self.copy(b, p, slot, self.where(p, 0, 0), c, pl_.device(ORDERS[p][0], (1, 3, 2)[slot]))
-        if slot < 11:
-            phase, k = 1 + (slot - 3) // 4, (slot - 3) % 4
-            step, half, to = ((0, None, 1), (0, None, 3), (-1, 0, 1), (1, 1, 3))[k]
-            return self.copy(b, p, slot, self.where(p, phase, step, half), c, pl_.device(ORDERS[p][phase], to))
-        step = (0, -1, 1, 2)[slot - 11]
-        return self.copy(b, p, slot, self.where(p, 2, step), c, pl_.device(core=1 - c))
-
-    def coming(self, b, p, slot):
-        pl_ = self.place
-        c = pl_.core
-        if slot < 3:
-            step = (-1, 1, 2)[slot]
-            return self.copy(b, p, slot, self.where(p, 0, step), c, pl_.device(ORDERS[p][0], (3, 1, 2)[slot]))
-        if slot < 11:
-            phase, k = 1 + (slot - 3) // 4, (slot - 3) % 4
-            step, half, to = ((-1, None, 3), (1, None, 1), (2, 0, 3), (2, 1, 1))[k]
-            return self.copy(b, p, slot, self.where(p, phase, step, half), c, pl_.device(ORDERS[p][phase], to))
-        step = (0, -1, 1, 2)[slot - 11]
-        return self.copy(b, p, slot, self.where(p, 2, step), 1 - c, pl_.device(core=1 - c))
-
-    STAGES = (
-        ((), (0, 1, 2)),
-        ((0, 1, 2), (3, 4)),
-        ((3, 4), (5, 6)),
-        ((5, 6), (7, 8, 11)),
-        ((7, 8), (9, 10, 12, 13)),
-        ((9, 10), (14,)),
-    )
-
-    def stage(self, b, k, parts=(0, 1, 2)):
-        waits, sends = self.STAGES[k]
-        for p in parts:
+                where[axis] = ("pair", half)
+        at = region(where, core)
+        return (slice(None) if block is None else block,) + at + (slice(None), columns)
+
+    def link(self, p, b, slot, coming):
+        c = self.place.core
+        full = slice(None)
+        if b is None:
+            phase, at = 0, slot
+        elif slot < 3:
+            phase, at = 1, 3 + b * SLOTS + slot
+        else:
+            phase, at = 2, 3 + b * SLOTS + slot
+        axis = ORDERS[p][phase]
+        if b is None or slot < 6:
+            k = slot % 3
+            to = STEPS[k]
+            columns = EARLY if phase == 2 else full
+            step = (4 - to) % 4 if coming else 0
+            return self.copy(p, at, self.index(p, b, phase, step, c, columns), self.place.device(axis, to))
+        if slot in (7, 8):
+            to = STEPS[slot - 7]
+            step = (4 - to) if coming else 0
+            return self.copy(p, at, self.index(p, b, 2, step, c, LATE), self.place.device(axis, to))
+        if slot in (9, 10):
+            to = STEPS[slot - 9]
+            step = 2 if coming else 4 - to
+            return self.copy(p, at, self.index(p, b, 2, step, c, LATE, slot - 9), self.place.device(axis, to))
+        c = 1 - c if coming else c
+        other = self.place.device(core=1 - self.place.core)
+        if slot == 6:
+            return self.copy(p, at, self.index(p, b, 2, None, c, EARLY), other)
+        return self.copy(p, at, self.index(p, b, 2, ("pair", slot - 11), c, LATE), other)
+
+    def start(self, b, slots):
+        for p in range(3):
+            for slot in slots:
+                self.link(p, b, slot, False).start()
+
+    def wait(self, b, slots):
+        for p in range(3):
+            for slot in slots:
+                self.link(p, b, slot, True).wait_recv()
+
+    def step(self, b, waits, sends):
+        for p in range(3):
             for slot in waits:
-                self.coming(b, p, slot).wait_recv()
+                self.link(p, b, slot, True).wait_recv()
             for slot in sends:
-                self.going(b, p, slot).start()
-
-    def finish(self, b, parts=(0, 1, 2)):
-        for p in parts:
-            for slot in (11, 12, 13, 14):
-                self.coming(b, p, slot).wait_recv()
-
-    def drain(self, b, parts=(0, 1, 2)):
-        for p in parts:
-            for slot in range(15):
-                self.going(b, p, slot).wait_send()
+                self.link(p, b, slot, False).start()
+
+    def drain(self, b, slots):
+        for p in range(3):
+            for slot in slots:
+                self.link(p, b, slot, False).wait_send()
 
 
 def greet(place, more):
@@ -246,37 +257,45 @@
         self.gain_one = gain_one[b : b + 1, :]
         self.gain_two = gain_two[b : b + 1, :]
 
+    def tile(self, p, h, first, last):
+        return self.bufs[p][self.b, h, :, :, :, :, :, first:last].reshape(D, last - first)
+
     def attend(self, x, regions=None):
-        b, wa = self.b, self.bufs[0]
         n1 = layer_norm(x, self.gain_one)
-        qk = dot(n1, wa[b, 0].reshape(D, 1024)).astype(BF)
-        wv = wa[b, 1, :, :, :, :, :, 0:512].reshape(D, D)
-        v = dot(n1, wv).astype(BF)
+        q, k, v = [
+            jnp.concatenate([dot(n1, self.tile(p, h, 0, 256)).astype(BF) for h in range(2)], 1) for p in range(3)
+        ]
         out = []
         for w in range(2):
             rows = slice(w * 144, (w + 1) * 144)
             mask = None
             if regions is not None:
                 kinds = lax.broadcasted_iota(jnp.int32, (8, 144), 0)
-                ids = jnp.broadcast_to(regions[w : w + 1, :], (8, 144))
+                ids = jnp.broadcast_to(regions[w], (8, 144))
                 hot = (kinds == ids).astype(F32).astype(BF)
                 same = dot(hot, hot, ((0,), (0,)))
                 mask = jnp.concatenate([same] * 4, 1) > 0.5
-            out.append(attention(qk[rows, 0:D], qk[rows, D : 2 * D], v[rows], mask))
+            out.append(attention(q[rows], k[rows], v[rows], mask))
         return jnp.concatenate(out, 0)
 
     def mix(self, x, context):
-        wp = self.bufs[0][self.b, 1, :, :, :, :, :, 512:1024].reshape(D, D)
-        return (x + dot(context, wp)).astype(BF).astype(F32)
+        added = [dot(context, self.tile(1, h, 512, 768)) for h in range(2)]
+        return (x + jnp.concatenate(added, 1)).astype(BF).astype(F32)
 
     def feed(self, mixed):
         b = self.b
         n2 = layer_norm(mixed, self.gain_two)
         sums = [0.0, 0.0]
         for h in range(2):
-            hidden = gelu(dot(n2, self.bufs[1][b, h].reshape(D, 1024))).astype(BF)
+            up = [dot(n2, self.tile(0, h, 256, 1024)), dot(n2, self.tile(1, h, 256, 512))]
+            hidden = jnp.concatenate([gelu(u).astype(BF) for u in up], 1)
             for side in range(2):
-                wd = self.bufs[2][b, side, 2 * h : 2 * h + 2].reshape(1024, 256)
+                lines = [self.bufs[1][b, side, 2 * h : 2 * h + 2, :, :, :, :, 768:1024]]
+                for i in range(1, 4):
+                    lines.append(
+                        self.bufs[2][b, side, 2 * h : 2 * h + 2, :, :, :, :, 256 * i : 256 * i + 256]
+                    )
+                wd = jnp.stack([line.reshape(32, 8, 256) for line in lines], 1).reshape(1024, 256)
                 sums[side] = sums[side] + dot(hidden, wd)
         return (mixed + jnp.concatenate(sums, 1)).astype(BF)
 
@@ -297,9 +316,6 @@
     tokens,
     level_table,
     latent_query,
-    w_query,
-    w_kv,
-    w_attn_out,
     regions,
     gain_one,
     gain_two,
@@ -307,11 +323,15 @@
     w_proj,
     w_up,
     w_down,
-    spread,
     halves,
-    cut,
-    roll_rows,
-    back_rows,
+    columns,
+    w_query_h,
+    w_kv_h,
+    w_attn_out_h,
+    spread_h,
+    cut_h,
+    roll_rows_h,
+    back_rows_h,
     out,
     ba,
     bb,
@@ -323,6 +343,13 @@
     hr,
     hs2,
     hr2,
+    w_query,
+    w_kv,
+    w_attn_out,
+    spread,
+    cut,
+    roll_rows,
+    back_rows,
     send,
     recv,
     tok_sem,
@@ -330,24 +357,41 @@
     hrsem,
     h2sem,
     h2rsem,
+    load_sem,
 ):
     place = Place()
     lev, lat = place.lev, place.lat
     partner = (1 - lev, lat)
     ahead, behind = lax.rem(lat + 1, 64), lax.rem(lat + 63, 64)
     barrier, count = greet(place, [(lev, ahead), (lev, behind), (1 - lev, ahead), (1 - lev, behind)])
+    pairs = (
+        (w_query_h, w_query),
+        (w_kv_h, w_kv),
+        (spread_h, spread),
+        (w_attn_out_h, w_attn_out),
+        (cut_h, cut),
+        (roll_rows_h, roll_rows),
+        (back_rows_h, back_rows),
+    )
+    loads = [pltpu.make_async_copy(src, dst, load_sem.at[n]) for n, (src, dst) in enumerate(pairs)]
+    for load in loads:
+        load.start()
     bufs = (ba, bb, bc)
     g = Gather(place, bufs, send, recv)
     first = lev == 0
+
+    def half(array, start, width, apart):
+        return jnp.where(first, array[:, start : start + width], array[:, start + apart : start + apart + width])
+
     for blk in range(2):
         at = (blk,) + region(place.pos, place.core)
-        qkv = w_qkv[blk]
-        proj = w_proj[blk]
-        ba[at] = jnp.where(first, qkv[:, 0:1024], jnp.concatenate([qkv[:, 1024:1536], proj], 1))
-        up = w_up[blk]
-        bb[at] = jnp.where(first, up[:, 0:1024], up[:, 1024:2048])
-        down = w_down[blk]
-        bc[at] = jnp.where(first, down[:, 0:256], down[:, 256:512])
+        qkv, up, down = w_qkv[blk], w_up[blk], half(w_down[blk], 0, 256, 256)
+        lines = [down[8 * i : 8 * i + 8] for i in range(4)]
+        ba[at] = jnp.concatenate([half(qkv, 0, 256, 256), half(up, 0, 768, 1024)], 1)
+        bb[at] = jnp.concatenate(
+            [half(qkv, 512, 256, 256), half(up, 768, 256, 1024), half(w_proj[blk], 0, 256, 256), lines[0]], 1
+        )
+        bc[at] = jnp.concatenate([half(qkv, 1024, 256, 256)] + lines[1:], 1)
     select = halves[lev]
     for slot in range(4):
         row = level_table[pl.ds(level_ids[slot], 1), :]
@@ -357,18 +401,23 @@
         tok_send[slot] = both[PAD : 2 * PAD]
     pl.semaphore_wait(barrier, count)
 
-    g.stage(0, 0)
-    tok = pltpu.make_async_remote_copy(
-        src_ref=tok_send,
-        dst_ref=tok_recv,
-        send_sem=tok_sem.at[0],
-        recv_sem=tok_sem.at[1],
-        device_id=partner,
-        device_id_type=MESH,
-    )
-    tok.start()
-    g.stage(1, 0)
-
+    g.start(None, (0, 1, 2))
+    toks = [
+        pltpu.make_async_remote_copy(
+            src_ref=tok_send.at[pl.ds(2 * n, 2)],
+            dst_ref=tok_recv.at[pl.ds(2 * n, 2)],
+            send_sem=tok_sem.at[2 * n],
+            recv_sem=tok_sem.at[2 * n + 1],
+            device_id=partner,
+            device_id_type=MESH,
+        )
+        for n in range(2)
+    ]
+    toks[0].start()
+
+    loads[0].wait()
+    loads[1].wait()
+    loads[2].wait()
     queries = dot(latent_query[...], w_query[...]).astype(BF).astype(F32)
     wide_q = jnp.concatenate(
         [jnp.broadcast_to(queries[q : q + 1], (HEADS, D)) for q in range(Q_LAT)], 0
@@ -380,14 +429,16 @@
         score = dot(kv[:, 0:D], query_block, ((1,), (1,)))
         return score.reshape(4, PAD, Q_LAT * HEADS), kv[:, D : 2 * D].astype(F32).reshape(4, PAD, D)
 
+    g.step(None, (0, 1, 2), ())
+    g.start(0, (0, 1, 2))
+    toks[1].start()
+    g.start(1, (0, 1, 2))
     score_own, val_own = keys_values(tok_own)
-    g.stage(0, 1)
-    g.stage(1, 1)
-    g.stage(0, 2)
-    g.stage(1, 2)
-    tok.wait_recv()
+    g.step(0, (0, 1, 2), (3, 4, 5))
+    g.start(0, (7, 8))
+    toks[0].wait_recv()
+    toks[1].wait_recv()
     score_par, val_par = keys_values(tok_recv)
-    g.stage(0, 3)
     top = jnp.maximum(jnp.max(score_own, 0), jnp.max(score_par, 0))
     w_own = jnp.exp2((score_own - top) * EXP_SCALE)
     w_par = jnp.exp2((score_par - top) * EXP_SCALE)
@@ -402,20 +453,30 @@
         total = jnp.sum(dot(w_own, owner).reshape(4, PAD, D) * val_own, 0)
         total = total + jnp.sum(dot(w_par, owner).reshape(4, PAD, D) * val_par, 0)
         attended.append(total[0:72])
-    g.stage(0, 4)
     attended = jnp.concatenate(attended, 0).astype(BF)
     base = jnp.concatenate([jnp.broadcast_to(queries[q : q + 1], (72, D)) for q in range(Q_LAT)], 0)
+    loads[3].wait()
     x = (dot(attended, w_attn_out[...]) + base).astype(BF).astype(F32)
-    g.stage(1, 3)
-    g.stage(0, 5)
-    g.finish(0)
+    g.step(0, (3, 4, 5), (6,))
+    g.wait(0, (6,))
 
     block = Block(0, bufs, gain_one, gain_two)
     context = block.attend(x)
-    g.stage(1, 4)
+    g.step(0, (7, 8), (9, 10, 11))
+    g.step(1, (0, 1, 2), (3, 4, 5))
+    g.start(1, (7, 8))
+    g.drain(None, (0, 1, 2))
+    g.drain(0, (0, 1, 2, 3, 4, 5, 6))
+    placed = dot(regions[0].astype(F32).astype(BF), columns[0])
+    for r in range(1, 6):
+        placed = placed + dot(regions[r].astype(F32).astype(BF), columns[r])
+    ids = placed.astype(jnp.int32)
+    labels = [jnp.concatenate([ids[2 * w : 2 * w + 1], ids[2 * w + 1 : 2 * w + 2]], 1) for w in range(2)]
+    g.step(0, (9, 10), (12,))
+    g.wait(0, (11, 12))
     mixed = block.mix(x, context)
     plain = block.feed(mixed)
-    g.stage(1, 5)
+    loads[4].wait()
     quarters = dot(cut[...], plain).astype(BF)
     for n in range(4):
         hs[n] = quarters[n * PAD : (n + 1) * PAD]
@@ -427,14 +488,21 @@
     ]
     for copy in sent:
         copy.start()
-    g.finish(1)
+    g.step(1, (3, 4, 5), (6,))
+    g.step(1, (7, 8), (9, 10, 11))
+    loads[5].wait()
     for copy in sent:
         copy.wait_recv()
     tiles = jnp.concatenate([hs[3], hr[0], hr[1], hr[2]], 0)
     x = dot(roll_rows[...], tiles)
+    g.wait(1, (6,))
 
     block = Block(1, bufs, gain_one, gain_two)
-    context = block.attend(x, regions)
+    context = block.attend(x, labels)
+    g.step(1, (9, 10), (12,))
+    g.drain(0, (7, 8, 9, 10, 11, 12))
+    g.drain(1, (0, 1, 2, 3, 4, 5, 6))
+    g.wait(1, (11, 12))
     mixed = block.mix(x, context)
     shifted = block.feed(mixed)
     quarters = dot(cut[...], shifted).astype(BF)
@@ -448,15 +516,17 @@
     ]
     for copy in back:
         copy.start()
+    for tok in toks:
+        tok.wait_send()
+    g.drain(1, (7, 8, 9, 10, 11, 12))
+    loads[6].wait()
+    for copy in sent:
+        copy.wait_send()
     for copy in back:
         copy.wait_recv()
     tiles = jnp.concatenate([hr2[2], hr2[1], hr2[0], hs2[0]], 0)
     out[...] = dot(back_rows[...], tiles).astype(BF)
-
-    tok.wait_send()
-    g.drain(0)
-    g.drain(1)
-    for copy in sent + back:
+    for copy in back:
         copy.wait_send()
 
 
@@ -476,20 +546,19 @@
     w_up,
     w_down,
 ):
-    labels = jnp.transpose(regions, (2, 0, 1)).reshape(2, 144)
+    place_row = np.stack([one_hot(12, 72, [(c, r * 12 + c) for c in range(12)]) for r in range(6)])
+    halves, cut, roll_rows, back_rows = [jnp.asarray(a) for a in row_orders()]
     vmem = pl.BlockSpec(memory_space=pltpu.VMEM)
-    consts = [jnp.asarray(head_spread())] + [jnp.asarray(a) for a in row_orders()]
+    whole = pl.BlockSpec(memory_space=pl.ANY)
     buf = pltpu.VMEM
     dma = pltpu.SemaphoreType.DMA
     flat = pl.pallas_call(
         kernel,
         out_shape=jax.ShapeDtypeStruct((288, D), BF),
-        in_specs=[pl.BlockSpec(memory_space=pltpu.SMEM)] + [vmem] * 18,
+        in_specs=[pl.BlockSpec(memory_space=pltpu.SMEM)] + [vmem] * 12 + [whole] * 7,
         out_specs=vmem,
-        scratch_shapes=[
-            buf((2, 2, 4, 4, 2, 2, 8, 1024), BF),
-            buf((2, 2, 4, 4, 2, 2, 8, 1024), BF),
-            buf((2, 2, 4, 4, 2, 2, 32, 256), BF),
+        scratch_shapes=[buf((2, 2, 4, 4, 2, 2, 8, 1024), BF)] * 3
+        + [
             buf((4, PAD, D), BF),
             buf((4, PAD, D), BF),
             buf((4, PAD, D), BF),
@@ -497,13 +566,21 @@
             buf((3, PAD, D), BF),
             buf((4, PAD, D), BF),
             buf((3, PAD, D), BF),
-            dma((2, 3, 15)),
-            dma((2, 3, 15)),
-            dma((2,)),
+            buf((D, D), BF),
+            buf((D, 2 * D), BF),
+            buf((D, D), BF),
+            buf((Q_LAT * HEADS, D), BF),
+            buf((4 * PAD, 288), BF),
+            buf((288, 4 * PAD), BF),
+            buf((288, 4 * PAD), BF),
+            dma((3, 3 + 2 * SLOTS)),
+            dma((3, 3 + 2 * SLOTS)),
+            dma((4,)),
             dma((3,)),
             dma((3,)),
             dma((3,)),
             dma((3,)),
+            dma((7,)),
         ],
         compiler_params=pltpu.CompilerParams(
             collective_id=0, has_side_effects=True, vmem_limit_bytes=56 << 20
@@ -514,17 +591,22 @@
         tokens,
         level_table,
         latent_query,
-        w_query,
-        w_kv,
-        w_attn_out,
-        labels,
+        jnp.transpose(regions, (0, 2, 1)),
         gain_one,
         gain_two,
         w_qkv,
         w_proj,
         w_up,
         w_down,
-        *consts,
+        halves,
+        jnp.asarray(place_row.astype(BF)),
+        w_query,
+        w_kv,
+        w_attn_out,
+        jnp.asarray(head_spread()),
+        cut,
+        roll_rows,
+        back_rows,
     )
     return flat.reshape(6, 12, Q_LAT, D)
 

time: 74 us -> 69 us (0.932)
  Pallas kernels: 70.6 us -> 67.1 us
  local copies, waits for them, and re-layouts: 3.12 us -> 1.75 us
    pallas_call x1, Pallas kernels: 70.6 us -> 67.1 us  [local(): pl.pallas_call(kernel, out_shape=jax.ShapeDtypeStruct((288, D), BF), in_s...]
where the time goes in v2:
time: 69 us; the launch traced here: 68.9 us
  Pallas kernels  67.1 us (97%)
  local copies, waits for them, and re-layouts  1.75 us (3%)
    pallas_call x1, Pallas kernels, local(): pl.pallas_call(kernel, out_shape=jax.ShapeDtypeStruct((288, D), BF), in_s...  67.1 us
    reshape x1, local copies, waits for them, and re-layouts, local(): return flat.reshape(6, 12, Q_LAT, D)  1.75 us

profile of v2, /device:TPU:0, one launch (start us, length us, event | category | flops | bytes accessed | tf_op | source)
XLA Modules:
  0.0 68.9 jit_solution(13073764126428023028)
XLA Ops:
  0.0 67.1 %encode_and_blocks.1 = bf16[288,512]{1,0:T(8,128)(2,1)} custom-call(s32[4]{0:T(128)} %level_ids.1, bf16[4,6,24,512]{3,2,1,0:T(8,128)(2,1)} %tokens.1, f32[13,512]{1,0:T(8,128)} %level_table.1, bf16[4,512]{1,0:T(4,128)(2,1)} %latent_query.1, s32[6,4,12]{2,1,0:T(4,128)} %bitcast.1, f32[2,512]{1,0:T(2,128)} %gain_one.1, f32[2,512]{1,0:T(2,128)} %gain_two.1, ...), custom_call_target="tpu_custom_call" | custom-call | tf_op jit(solution)/shard_map/encode_and_blocks/pallas_call | solution.py:555
  67.1 1.7 %reshape.3 = bf16[6,12,4,512]{3,2,1,0:T(4,128)(2,1)} reshape(bf16[288,512]{1,0:T(8,128)(2,1)} %encode_and_blocks.1) | data formatting | bytes 589824 | tf_op jit(solution)/shard_map/reshape | solution.py:611

commit v3 on v2

--- a/solution.py
+++ b/solution.py
@@ -12,7 +12,8 @@
 HD = 32
 Q_LAT = 4
 D = 512
-PAD = 80
+CELLS = 72
+TILES = CELLS // 8
 EPS = 1e-05
 BF = jnp.bfloat16
 F32 = jnp.float32
@@ -58,9 +59,9 @@
     return (xl, line(y), line(z), xh, core)
 
 
-SLOTS = 13
-EARLY = slice(0, 256)
-LATE = slice(256, 1024)
+SLOTS = 15
+EARLY = 256
+WIDTHS = (1152, 768, 1152)
 STEPS = (1, 3, 2)
 
 
@@ -98,7 +99,7 @@
 
     def link(self, p, b, slot, coming):
         c = self.place.core
-        full = slice(None)
+        full, early, late = slice(None), slice(0, EARLY), slice(EARLY, WIDTHS[p])
         if b is None:
             phase, at = 0, slot
         elif slot < 3:
@@ -109,26 +110,27 @@
         if b is None or slot < 6:
             k = slot % 3
             to = STEPS[k]
-            columns = EARLY if phase == 2 else full
+            columns = early if phase == 2 else full
             step = (4 - to) % 4 if coming else 0
             return self.copy(p, at, self.index(p, b, phase, step, c, columns), self.place.device(axis, to))
-        if slot in (7, 8):
-            to = STEPS[slot - 7]
+        if slot in (7, 8, 9, 10):
+            way, later = (slot - 7) // 2, (slot - 7) % 2
+            to = STEPS[way]
             step = (4 - to) if coming else 0
-            return self.copy(p, at, self.index(p, b, 2, step, c, LATE), self.place.device(axis, to))
-        if slot in (9, 10):
-            to = STEPS[slot - 9]
+            return self.copy(p, at, self.index(p, b, 2, step, c, late, way ^ later), self.place.device(axis, to))
+        if slot in (11, 12):
+            to = STEPS[slot - 11]
             step = 2 if coming else 4 - to
-            return self.copy(p, at, self.index(p, b, 2, step, c, LATE, slot - 9), self.place.device(axis, to))
+            return self.copy(p, at, self.index(p, b, 2, step, c, late, slot - 11), self.place.device(axis, to))
         c = 1 - c if coming else c
         other = self.place.device(core=1 - self.place.core)
         if slot == 6:
-            return self.copy(p, at, self.index(p, b, 2, None, c, EARLY), other)
-        return self.copy(p, at, self.index(p, b, 2, ("pair", slot - 11), c, LATE), other)
+            return self.copy(p, at, self.index(p, b, 2, None, c, early), other)
+        return self.copy(p, at, self.index(p, b, 2, ("pair", slot - 13), c, late), other)
 
     def start(self, b, slots):
-        for p in range(3):
-            for slot in slots:
+        for slot in slots:
+            for p in range(3):
                 self.link(p, b, slot, False).start()
 
     def wait(self, b, slots):
@@ -191,17 +193,17 @@
 
 
 def quarter_row(k, r, c):
-    return ((r // 3) * 2 + c // 6) * PAD + k * 18 + (r % 3) * 6 + c % 6
+    return ((r // 3) * 2 + c // 6) * CELLS + k * 18 + (r % 3) * 6 + c % 6
 
 
 def row_orders():
     halves = np.stack(
         [
             one_hot(
-                2 * PAD,
+                2 * CELLS,
                 144,
                 [
-                    (side * PAD + r * 12 + c, r * 24 + c + 12 * (lev ^ side))
+                    (side * CELLS + r * 12 + c, r * 24 + c + 12 * (lev ^ side))
                     for side in range(2)
                     for r in range(6)
                     for c in range(12)
@@ -210,12 +212,12 @@
             for lev in range(2)
         ]
     )
-    cut = one_hot(4 * PAD, 288, [(quarter_row(k, r, c), k * 72 + r * 12 + c) for k, r, c in cells()])
+    cut = one_hot(4 * CELLS, 288, [(quarter_row(k, r, c), k * 72 + r * 12 + c) for k, r, c in cells()])
     rolled = one_hot(
-        288, 4 * PAD, [(k * 72 + r * 12 + c, quarter_row((k + 1) % 4, r, c)) for k, r, c in cells()]
+        288, 4 * CELLS, [(k * 72 + r * 12 + c, quarter_row((k + 1) % 4, r, c)) for k, r, c in cells()]
     )
     back = one_hot(
-        288, 4 * PAD, [(r * 48 + c * 4 + (k + 1) % 4, quarter_row(k, r, c)) for k, r, c in cells()]
+        288, 4 * CELLS, [(r * 48 + c * 4 + (k + 1) % 4, quarter_row(k, r, c)) for k, r, c in cells()]
     )
     return [a.astype(BF) for a in (halves, cut, rolled, back)]
 
@@ -260,23 +262,22 @@
     def tile(self, p, h, first, last):
         return self.bufs[p][self.b, h, :, :, :, :, :, first:last].reshape(D, last - first)
 
-    def attend(self, x, regions=None):
+    def qkv(self, x):
         n1 = layer_norm(x, self.gain_one)
-        q, k, v = [
+        return [
             jnp.concatenate([dot(n1, self.tile(p, h, 0, 256)).astype(BF) for h in range(2)], 1) for p in range(3)
         ]
-        out = []
-        for w in range(2):
-            rows = slice(w * 144, (w + 1) * 144)
-            mask = None
-            if regions is not None:
-                kinds = lax.broadcasted_iota(jnp.int32, (8, 144), 0)
-                ids = jnp.broadcast_to(regions[w], (8, 144))
-                hot = (kinds == ids).astype(F32).astype(BF)
-                same = dot(hot, hot, ((0,), (0,)))
-                mask = jnp.concatenate([same] * 4, 1) > 0.5
-            out.append(attention(q[rows], k[rows], v[rows], mask))
-        return jnp.concatenate(out, 0)
+
+    def window(self, qkv, w, regions=None):
+        q, k, v = [part[w * 144 : (w + 1) * 144] for part in qkv]
+        mask = None
+        if regions is not None:
+            kinds = lax.broadcasted_iota(jnp.int32, (8, 144), 0)
+            ids = jnp.broadcast_to(regions[w], (8, 144))
+            hot = (kinds == ids).astype(F32).astype(BF)
+            same = dot(hot, hot, ((0,), (0,)))
+            mask = jnp.concatenate([same] * 4, 1) > 0.5
+        return attention(q, k, v, mask)
 
     def mix(self, x, context):
         added = [dot(context, self.tile(1, h, 512, 768)) for h in range(2)]
@@ -290,12 +291,14 @@
             up = [dot(n2, self.tile(0, h, 256, 1024)), dot(n2, self.tile(1, h, 256, 512))]
             hidden = jnp.concatenate([gelu(u).astype(BF) for u in up], 1)
             for side in range(2):
-                lines = [self.bufs[1][b, side, 2 * h : 2 * h + 2, :, :, :, :, 768:1024]]
-                for i in range(1, 4):
-                    lines.append(
-                        self.bufs[2][b, side, 2 * h : 2 * h + 2, :, :, :, :, 256 * i : 256 * i + 256]
-                    )
-                wd = jnp.stack([line.reshape(32, 8, 256) for line in lines], 1).reshape(1024, 256)
+
+                def line(p, first, width):
+                    part = self.bufs[p][b, side, 2 * h : 2 * h + 2, :, :, :, :, first : first + width]
+                    return part.reshape(32, 8, width)
+
+                lines = [jnp.concatenate([line(0, 1024, 128), line(2, 1024, 128)], 2)]
+                lines += [line(2, 256 * i, 256) for i in range(1, 4)]
+                wd = jnp.stack(lines, 1).reshape(1024, 256)
                 sums[side] = sums[side] + dot(hidden, wd)
         return (mixed + jnp.concatenate(sums, 1)).astype(BF)
 
@@ -313,26 +316,45 @@
 
 def kernel(
     level_ids,
-    tokens,
+    level_table_h,
+    latent_query_h,
+    regions_h,
+    gain_one_h,
+    gain_two_h,
+    tokens_h,
+    halves_h,
+    w_qkv_h,
+    w_proj_h,
+    w_up_h,
+    w_down_h,
+    w_query_h,
+    w_kv_h,
+    spread_h,
+    w_attn_out_h,
+    columns_h,
+    cut_h,
+    roll_rows_h,
+    back_rows_h,
+    out,
     level_table,
     latent_query,
     regions,
     gain_one,
     gain_two,
+    tokens,
+    halves,
     w_qkv,
     w_proj,
     w_up,
     w_down,
-    halves,
+    w_query,
+    w_kv,
+    spread,
+    w_attn_out,
     columns,
-    w_query_h,
-    w_kv_h,
-    w_attn_out_h,
-    spread_h,
-    cut_h,
-    roll_rows_h,
-    back_rows_h,
-    out,
+    cut,
+    roll_rows,
+    back_rows,
     ba,
     bb,
     bc,
@@ -343,13 +365,6 @@
     hr,
     hs2,
     hr2,
-    w_query,
-    w_kv,
-    w_attn_out,
-    spread,
-    cut,
-    roll_rows,
-    back_rows,
     send,
     recv,
     tok_sem,
@@ -365,10 +380,22 @@
     ahead, behind = lax.rem(lat + 1, 64), lax.rem(lat + 63, 64)
     barrier, count = greet(place, [(lev, ahead), (lev, behind), (1 - lev, ahead), (1 - lev, behind)])
     pairs = (
+        (w_qkv_h, w_qkv),
+        (w_proj_h, w_proj),
+        (w_up_h, w_up),
+        (w_down_h, w_down),
+        (level_table_h, level_table),
+        (tokens_h, tokens),
+        (halves_h, halves),
+        (latent_query_h, latent_query),
         (w_query_h, w_query),
+        (spread_h, spread),
         (w_kv_h, w_kv),
-        (spread_h, spread),
         (w_attn_out_h, w_attn_out),
+        (gain_one_h, gain_one),
+        (gain_two_h, gain_two),
+        (regions_h, regions),
+        (columns_h, columns),
         (cut_h, cut),
         (roll_rows_h, roll_rows),
         (back_rows_h, back_rows),
@@ -376,6 +403,11 @@
     loads = [pltpu.make_async_copy(src, dst, load_sem.at[n]) for n, (src, dst) in enumerate(pairs)]
     for load in loads:
         load.start()
+
+    def loaded(first, last):
+        for load in loads[first:last]:
+            load.wait()
+
     bufs = (ba, bb, bc)
     g = Gather(place, bufs, send, recv)
     first = lev == 0
@@ -383,22 +415,24 @@
     def half(array, start, width, apart):
         return jnp.where(first, array[:, start : start + width], array[:, start + apart : start + apart + width])
 
+    loaded(0, 4)
     for blk in range(2):
         at = (blk,) + region(place.pos, place.core)
         qkv, up, down = w_qkv[blk], w_up[blk], half(w_down[blk], 0, 256, 256)
         lines = [down[8 * i : 8 * i + 8] for i in range(4)]
-        ba[at] = jnp.concatenate([half(qkv, 0, 256, 256), half(up, 0, 768, 1024)], 1)
+        ba[at] = jnp.concatenate([half(qkv, 0, 256, 256), half(up, 0, 768, 1024), lines[0][:, 0:128]], 1)
         bb[at] = jnp.concatenate(
-            [half(qkv, 512, 256, 256), half(up, 768, 256, 1024), half(w_proj[blk], 0, 256, 256), lines[0]], 1
+            [half(qkv, 512, 256, 256), half(up, 768, 256, 1024), half(w_proj[blk], 0, 256, 256)], 1
         )
-        bc[at] = jnp.concatenate([half(qkv, 1024, 256, 256)] + lines[1:], 1)
+        bc[at] = jnp.concatenate([half(qkv, 1024, 256, 256)] + lines[1:] + [lines[0][:, 128:256]], 1)
+    loaded(4, 7)
     select = halves[lev]
     for slot in range(4):
         row = level_table[pl.ds(level_ids[slot], 1), :]
         summed = (tokens[slot].astype(F32).reshape(144, D) + row).astype(BF)
-        both = dot(select, summed).astype(BF)
-        tok_own[slot] = both[0:PAD]
-        tok_send[slot] = both[PAD : 2 * PAD]
+        both = dot(select, summed)
+        tok_own[slot] = both[0:CELLS].reshape(TILES, 8, D).astype(BF)
+        tok_send[slot] = both[CELLS : 2 * CELLS].reshape(TILES, 8, D).astype(BF)
     pl.semaphore_wait(barrier, count)
 
     g.start(None, (0, 1, 2))
@@ -415,9 +449,7 @@
     ]
     toks[0].start()
 
-    loads[0].wait()
-    loads[1].wait()
-    loads[2].wait()
+    loaded(7, 11)
     queries = dot(latent_query[...], w_query[...]).astype(BF).astype(F32)
     wide_q = jnp.concatenate(
         [jnp.broadcast_to(queries[q : q + 1], (HEADS, D)) for q in range(Q_LAT)], 0
@@ -425,9 +457,9 @@
     query_block = (wide_q * spread[...].astype(F32)).astype(BF)
 
     def keys_values(ref):
-        kv = dot(ref[...].astype(F32).reshape(4 * PAD, D).astype(BF), w_kv[...]).astype(BF)
+        kv = dot(ref[...].reshape(4 * CELLS, D), w_kv[...]).astype(BF)
         score = dot(kv[:, 0:D], query_block, ((1,), (1,)))
-        return score.reshape(4, PAD, Q_LAT * HEADS), kv[:, D : 2 * D].astype(F32).reshape(4, PAD, D)
+        return score.reshape(4, CELLS, Q_LAT * HEADS), kv[:, D : 2 * D].astype(F32).reshape(4, CELLS, D)
 
     g.step(None, (0, 1, 2), ())
     g.start(0, (0, 1, 2))
@@ -435,7 +467,7 @@
     g.start(1, (0, 1, 2))
     score_own, val_own = keys_values(tok_own)
     g.step(0, (0, 1, 2), (3, 4, 5))
-    g.start(0, (7, 8))
+    g.start(0, (7, 9, 8, 10))
     toks[0].wait_recv()
     toks[1].wait_recv()
     score_par, val_par = keys_values(tok_recv)
@@ -443,28 +475,33 @@
     w_own = jnp.exp2((score_own - top) * EXP_SCALE)
     w_par = jnp.exp2((score_par - top) * EXP_SCALE)
     inverse = 1.0 / (jnp.sum(w_own, 0) + jnp.sum(w_par, 0))
-    w_own = (w_own * inverse).reshape(4 * PAD, Q_LAT * HEADS).astype(BF)
-    w_par = (w_par * inverse).reshape(4 * PAD, Q_LAT * HEADS).astype(BF)
+    w_own = (w_own * inverse).reshape(4 * CELLS, Q_LAT * HEADS).astype(BF)
+    w_par = (w_par * inverse).reshape(4 * CELLS, Q_LAT * HEADS).astype(BF)
     attended = []
     line = lax.broadcasted_iota(jnp.int32, (Q_LAT * HEADS, D), 0)
     for q in range(Q_LAT):
         mine = (line >= q * HEADS) & (line < (q + 1) * HEADS)
         owner = jnp.where(mine, spread[...], jnp.zeros((Q_LAT * HEADS, D), BF))
-        total = jnp.sum(dot(w_own, owner).reshape(4, PAD, D) * val_own, 0)
-        total = total + jnp.sum(dot(w_par, owner).reshape(4, PAD, D) * val_par, 0)
-        attended.append(total[0:72])
+        total = jnp.sum(dot(w_own, owner).reshape(4, CELLS, D) * val_own, 0)
+        total = total + jnp.sum(dot(w_par, owner).reshape(4, CELLS, D) * val_par, 0)
+        attended.append(total)
     attended = jnp.concatenate(attended, 0).astype(BF)
-    base = jnp.concatenate([jnp.broadcast_to(queries[q : q + 1], (72, D)) for q in range(Q_LAT)], 0)
-    loads[3].wait()
+    base = jnp.concatenate([jnp.broadcast_to(queries[q : q + 1], (CELLS, D)) for q in range(Q_LAT)], 0)
+    loaded(11, 16)
     x = (dot(attended, w_attn_out[...]) + base).astype(BF).astype(F32)
     g.step(0, (3, 4, 5), (6,))
     g.wait(0, (6,))
 
     block = Block(0, bufs, gain_one, gain_two)
-    context = block.attend(x)
-    g.step(0, (7, 8), (9, 10, 11))
+    qkv = block.qkv(x)
+    g.step(0, (7, 9), (11, 12))
     g.step(1, (0, 1, 2), (3, 4, 5))
-    g.start(1, (7, 8))
+    g.start(1, (7, 9, 8, 10))
+    context = [block.window(qkv, 0)]
+    g.step(0, (8, 10), (13,))
+    context.append(block.window(qkv, 1))
+    context = jnp.concatenate(context, 0)
+    g.step(0, (11, 12), (14,))
     g.drain(None, (0, 1, 2))
     g.drain(0, (0, 1, 2, 3, 4, 5, 6))
     placed = dot(regions[0].astype(F32).astype(BF), columns[0])
@@ -472,59 +509,55 @@
         placed = placed + dot(regions[r].astype(F32).astype(BF), columns[r])
     ids = placed.astype(jnp.int32)
     labels = [jnp.concatenate([ids[2 * w : 2 * w + 1], ids[2 * w + 1 : 2 * w + 2]], 1) for w in range(2)]
-    g.step(0, (9, 10), (12,))
-    g.wait(0, (11, 12))
+    loaded(16, 19)
+    g.wait(0, (13, 14))
     mixed = block.mix(x, context)
     plain = block.feed(mixed)
-    loads[4].wait()
-    quarters = dot(cut[...], plain).astype(BF)
-    for n in range(4):
-        hs[n] = quarters[n * PAD : (n + 1) * PAD]
+    hs[...] = dot(cut[...], plain).reshape(4, TILES, 8, D).astype(BF)
     sems = (hsem, hrsem)
     sent = [
+        moved(hs, hr, sems, 1, (lev, behind), 1),
         moved(hs, hr, sems, 0, partner, 2),
-        moved(hs, hr, sems, 1, (lev, behind), 1),
         moved(hs, hr, sems, 2, (1 - lev, behind), 0),
     ]
     for copy in sent:
         copy.start()
     g.step(1, (3, 4, 5), (6,))
-    g.step(1, (7, 8), (9, 10, 11))
-    loads[5].wait()
+    g.step(1, (7, 9), (11, 12))
+    g.step(1, (8, 10), (13,))
     for copy in sent:
         copy.wait_recv()
-    tiles = jnp.concatenate([hs[3], hr[0], hr[1], hr[2]], 0)
+    tiles = jnp.concatenate([part.reshape(CELLS, D) for part in (hs[3], hr[0], hr[1], hr[2])], 0)
     x = dot(roll_rows[...], tiles)
     g.wait(1, (6,))
 
     block = Block(1, bufs, gain_one, gain_two)
-    context = block.attend(x, labels)
-    g.step(1, (9, 10), (12,))
-    g.drain(0, (7, 8, 9, 10, 11, 12))
-    g.drain(1, (0, 1, 2, 3, 4, 5, 6))
-    g.wait(1, (11, 12))
+    qkv = block.qkv(x)
+    context = [block.window(qkv, 0, labels)]
+    g.step(1, (11, 12), (14,))
+    context.append(block.window(qkv, 1, labels))
+    context = jnp.concatenate(context, 0)
+    g.wait(1, (13, 14))
     mixed = block.mix(x, context)
     shifted = block.feed(mixed)
-    quarters = dot(cut[...], shifted).astype(BF)
-    for n in range(4):
-        hs2[n] = quarters[n * PAD : (n + 1) * PAD]
+    hs2[...] = dot(cut[...], shifted).reshape(4, TILES, 8, D).astype(BF)
     sems = (h2sem, h2rsem)
     back = [
+        moved(hs2, hr2, sems, 1, (lev, ahead), 2),
         moved(hs2, hr2, sems, 0, partner, 1),
-        moved(hs2, hr2, sems, 1, (lev, ahead), 2),
         moved(hs2, hr2, sems, 2, (1 - lev, ahead), 3),
     ]
     for copy in back:
         copy.start()
     for tok in toks:
         tok.wait_send()
-    g.drain(1, (7, 8, 9, 10, 11, 12))
-    loads[6].wait()
+    g.drain(0, (7, 8, 9, 10, 11, 12, 13, 14))
+    g.drain(1, range(SLOTS))
     for copy in sent:
         copy.wait_send()
     for copy in back:
         copy.wait_recv()
-    tiles = jnp.concatenate([hr2[2], hr2[1], hr2[0], hs2[0]], 0)
+    tiles = jnp.concatenate([part.reshape(CELLS, D) for part in (hr2[2], hr2[1], hr2[0], hs2[0])], 0)
     out[...] = dot(back_rows[...], tiles).astype(BF)
     for copy in back:
         copy.wait_send()
@@ -548,31 +581,39 @@
 ):
     place_row = np.stack([one_hot(12, 72, [(c, r * 12 + c) for c in range(12)]) for r in range(6)])
     halves, cut, roll_rows, back_rows = [jnp.asarray(a) for a in row_orders()]
-    vmem = pl.BlockSpec(memory_space=pltpu.VMEM)
-    whole = pl.BlockSpec(memory_space=pl.ANY)
+    operands = (
+        level_table,
+        latent_query,
+        jnp.transpose(regions, (0, 2, 1)),
+        gain_one,
+        gain_two,
+        tokens,
+        halves,
+        w_qkv,
+        w_proj,
+        w_up,
+        w_down,
+        w_query,
+        w_kv,
+        jnp.asarray(head_spread()),
+        w_attn_out,
+        jnp.asarray(place_row.astype(BF)),
+        cut,
+        roll_rows,
+        back_rows,
+    )
     buf = pltpu.VMEM
     dma = pltpu.SemaphoreType.DMA
     flat = pl.pallas_call(
         kernel,
         out_shape=jax.ShapeDtypeStruct((288, D), BF),
-        in_specs=[pl.BlockSpec(memory_space=pltpu.SMEM)] + [vmem] * 12 + [whole] * 7,
-        out_specs=vmem,
-        scratch_shapes=[buf((2, 2, 4, 4, 2, 2, 8, 1024), BF)] * 3
+        in_specs=[pl.BlockSpec(memory_space=pltpu.SMEM)]
+        + [pl.BlockSpec(memory_space=pl.ANY)] * len(operands),
+        out_specs=pl.BlockSpec(memory_space=pltpu.VMEM),
+        scratch_shapes=[buf(a.shape, a.dtype) for a in operands]
+        + [buf((2, 2, 4, 4, 2, 2, 8, width), BF) for width in WIDTHS]
+        + [buf((n, TILES, 8, D), BF) for n in (4, 4, 4, 4, 3, 4, 3)]
         + [
-            buf((4, PAD, D), BF),
-            buf((4, PAD, D), BF),
-            buf((4, PAD, D), BF),
-            buf((4, PAD, D), BF),
-            buf((3, PAD, D), BF),
-            buf((4, PAD, D), BF),
-            buf((3, PAD, D), BF),
-            buf((D, D), BF),
-            buf((D, 2 * D), BF),
-            buf((D, D), BF),
-            buf((Q_LAT * HEADS, D), BF),
-            buf((4 * PAD, 288), BF),
-            buf((288, 4 * PAD), BF),
-            buf((288, 4 * PAD), BF),
             dma((3, 3 + 2 * SLOTS)),
             dma((3, 3 + 2 * SLOTS)),
             dma((4,)),
@@ -580,34 +621,13 @@
             dma((3,)),
             dma((3,)),
             dma((3,)),
-            dma((7,)),
+            dma((len(operands),)),
         ],
         compiler_params=pltpu.CompilerParams(
             collective_id=0, has_side_effects=True, vmem_limit_bytes=56 << 20
         ),
         name="encode_and_blocks",
-    )(
-        level_ids,
-        tokens,
-        level_table,
-        latent_query,
-        jnp.transpose(regions, (0, 2, 1)),
-        gain_one,
-        gain_two,
-        w_qkv,
-        w_proj,
-        w_up,
-        w_down,
-        halves,
-        jnp.asarray(place_row.astype(BF)),
-        w_query,
-        w_kv,
-        w_attn_out,
-        jnp.asarray(head_spread()),
-        cut,
-        roll_rows,
-        back_rows,
-    )
+    )(level_ids, *operands)
     return flat.reshape(6, 12, Q_LAT, D)
 
 

time: 69 us -> 64.7 us (0.938)
  Pallas kernels: 67.1 us -> 62.8 us
    pallas_call x1, Pallas kernels: 67.1 us -> 62.8 us  [local(): pl.pallas_call(kernel, out_shape=jax.ShapeDtypeStruct((288, D), BF), in_s...]
where the time goes in v3:
time: 64.7 us; the launch traced here: 64.6 us
  Pallas kernels  62.8 us (97%)
  local copies, waits for them, and re-layouts  1.75 us (3%)
    pallas_call x1, Pallas kernels, local(): pl.pallas_call(kernel, out_shape=jax.ShapeDtypeStruct((288, D), BF), in_s...  62.8 us
    reshape x1, local copies, waits for them, and re-layouts, local(): return flat.reshape(6, 12, Q_LAT, D)  1.75 us

profile of v3, /device:TPU:0, one launch (start us, length us, event | category | flops | bytes accessed | tf_op | source)
XLA Modules:
  0.0 64.6 jit_solution(3447903858072871606)
XLA Ops:
  0.0 62.8 %encode_and_blocks.1 = bf16[288,512]{1,0:T(8,128)(2,1)} custom-call(s32[4]{0:T(128)} %level_ids.1, f32[13,512]{1,0:T(8,128)} %level_table_h.1, bf16[4,512]{1,0:T(4,128)(2,1)} %latent_query_h.1, s32[6,4,12]{2,1,0:T(4,128)} %bitcast.1, f32[2,512]{1,0:T(2,128)} %gain_one_h.1, f32[2,512]{1,0:T(2,128)} %gain_two_h.1, bf16[4,6,24,512]{3,2,1,0:T(8,128)(2,1)} %tokens_h.1, ...), custom_call_target="tpu_custom_call" | custom-call | tf_op jit(solution)/shard_map/encode_and_blocks/pallas_call | solution.py:607
  62.8 1.7 %reshape.3 = bf16[6,12,4,512]{3,2,1,0:T(4,128)(2,1)} reshape(bf16[288,512]{1,0:T(8,128)(2,1)} %encode_and_blocks.1) | data formatting | bytes 589824 | tf_op jit(solution)/shard_map/reshape | solution.py:631

commit v4 on v3

--- a/solution.py
+++ b/solution.py
@@ -425,6 +425,9 @@
             [half(qkv, 512, 256, 256), half(up, 768, 256, 1024), half(w_proj[blk], 0, 256, 256)], 1
         )
         bc[at] = jnp.concatenate([half(qkv, 1024, 256, 256)] + lines[1:] + [lines[0][:, 128:256]], 1)
+    pl.semaphore_wait(barrier, count)
+
+    g.start(None, (0, 1, 2))
     loaded(4, 7)
     select = halves[lev]
     for slot in range(4):
@@ -433,9 +436,6 @@
         both = dot(select, summed)
         tok_own[slot] = both[0:CELLS].reshape(TILES, 8, D).astype(BF)
         tok_send[slot] = both[CELLS : 2 * CELLS].reshape(TILES, 8, D).astype(BF)
-    pl.semaphore_wait(barrier, count)
-
-    g.start(None, (0, 1, 2))
     toks = [
         pltpu.make_async_remote_copy(
             src_ref=tok_send.at[pl.ds(2 * n, 2)],
@@ -464,10 +464,10 @@
     g.step(None, (0, 1, 2), ())
     g.start(0, (0, 1, 2))
     toks[1].start()
-    g.start(1, (0, 1, 2))
     score_own, val_own = keys_values(tok_own)
     g.step(0, (0, 1, 2), (3, 4, 5))
     g.start(0, (7, 9, 8, 10))
+    g.start(1, (0, 1, 2))
     toks[0].wait_recv()
     toks[1].wait_recv()
     score_par, val_par = keys_values(tok_recv)
@@ -493,12 +493,12 @@
     g.wait(0, (6,))
 
     block = Block(0, bufs, gain_one, gain_two)
+    g.step(0, (7, 9), (11, 12))
     qkv = block.qkv(x)
-    g.step(0, (7, 9), (11, 12))
+    context = [block.window(qkv, 0)]
+    g.step(0, (8, 10), (13,))
     g.step(1, (0, 1, 2), (3, 4, 5))
     g.start(1, (7, 9, 8, 10))
-    context = [block.window(qkv, 0)]
-    g.step(0, (8, 10), (13,))
     context.append(block.window(qkv, 1))
     context = jnp.concatenate(context, 0)
     g.step(0, (11, 12), (14,))

time: 64.7 us -> 61.3 us (0.947)
  Pallas kernels: 62.8 us -> 59.1 us
    pallas_call x1, Pallas kernels: 62.8 us -> 59.1 us  [local(): pl.pallas_call(kernel, out_shape=jax.ShapeDtypeStruct((288, D), BF), in_s...]
where the time goes in v4:
time: 61.3 us; the launch traced here: 60.8 us
  Pallas kernels  59.1 us (96%)
  local copies, waits for them, and re-layouts  1.75 us (3%)
    pallas_call x1, Pallas kernels, local(): pl.pallas_call(kernel, out_shape=jax.ShapeDtypeStruct((288, D), BF), in_s...  59.1 us
    reshape x1, local copies, waits for them, and re-layouts, local(): return flat.reshape(6, 12, Q_LAT, D)  1.75 us

profile of v4, /device:TPU:0, one launch (start us, length us, event | category | flops | bytes accessed | tf_op | source)
XLA Modules:
  0.0 60.8 jit_solution(8157130478373506953)
XLA Ops:
  0.0 59.1 %encode_and_blocks.1 = bf16[288,512]{1,0:T(8,128)(2,1)} custom-call(s32[4]{0:T(128)} %level_ids.1, f32[13,512]{1,0:T(8,128)} %level_table_h.1, bf16[4,512]{1,0:T(4,128)(2,1)} %latent_query_h.1, s32[6,4,12]{2,1,0:T(4,128)} %bitcast.1, f32[2,512]{1,0:T(2,128)} %gain_one_h.1, f32[2,512]{1,0:T(2,128)} %gain_two_h.1, bf16[4,6,24,512]{3,2,1,0:T(8,128)(2,1)} %tokens_h.1, ...), custom_call_target="tpu_custom_call" | custom-call | tf_op jit(solution)/shard_map/encode_and_blocks/pallas_call | solution.py:607
  59.1 1.7 %reshape.3 = bf16[6,12,4,512]{3,2,1,0:T(4,128)(2,1)} reshape(bf16[288,512]{1,0:T(8,128)(2,1)} %encode_and_blocks.1) | data formatting | bytes 589824 | tf_op jit(solution)/shard_map/reshape | solution.py:631

commit v5 on v4

--- a/solution.py
+++ b/solution.py
@@ -14,6 +14,7 @@
 D = 512
 CELLS = 72
 TILES = CELLS // 8
+PART = 40
 EPS = 1e-05
 BF = jnp.bfloat16
 F32 = jnp.float32
@@ -59,7 +60,7 @@
     return (xl, line(y), line(z), xh, core)
 
 
-SLOTS = 15
+SLOTS = 20
 EARLY = 256
 WIDTHS = (1152, 768, 1152)
 STEPS = (1, 3, 2)
@@ -85,10 +86,7 @@
         where = [None, None, None]
         for k, axis in enumerate(order):
             if k == phase:
-                if isinstance(step, tuple):
-                    own = self.place.pos[axis] // 2
-                    where[axis] = ("pair", own if step[1] == 0 else 1 - own)
-                elif step is not None:
+                if step is not None:
                     where[axis] = lax.rem(self.place.pos[axis] + step, 4)
             elif k > phase:
                 where[axis] = self.place.pos[axis]
@@ -101,16 +99,20 @@
         c = self.place.core
         full, early, late = slice(None), slice(0, EARLY), slice(EARLY, WIDTHS[p])
         if b is None:
-            phase, at = 0, slot
+            phase, at, b = 0, slot, 0
+        elif 15 <= slot <= 17:
+            phase, at = 1 - b, 3 + b * SLOTS + slot
         elif slot < 3:
             phase, at = 1, 3 + b * SLOTS + slot
         else:
             phase, at = 2, 3 + b * SLOTS + slot
         axis = ORDERS[p][phase]
-        if b is None or slot < 6:
+        if phase == 0 or slot < 6 or 15 <= slot <= 17:
             k = slot % 3
             to = STEPS[k]
-            columns = early if phase == 2 else full
+            columns = full
+            if phase == 2 or (b == 0 and phase == 1):
+                columns = late if slot < 3 else early
             step = (4 - to) % 4 if coming else 0
             return self.copy(p, at, self.index(p, b, phase, step, c, columns), self.place.device(axis, to))
         if slot in (7, 8, 9, 10):
@@ -126,7 +128,8 @@
         other = self.place.device(core=1 - self.place.core)
         if slot == 6:
             return self.copy(p, at, self.index(p, b, 2, None, c, early), other)
-        return self.copy(p, at, self.index(p, b, 2, ("pair", slot - 13), c, late), other)
+        step = {13: 0, 14: 2, 18: 3, 19: 1}[slot]
+        return self.copy(p, at, self.index(p, b, 2, step, c, late), other)
 
     def start(self, b, slots):
         for slot in slots:
@@ -193,7 +196,7 @@
 
 
 def quarter_row(k, r, c):
-    return ((r // 3) * 2 + c // 6) * CELLS + k * 18 + (r % 3) * 6 + c % 6
+    return (((r // 3) * 2 + c // 6) * 2 + k // 2) * PART + (k % 2) * 18 + (r % 3) * 6 + c % 6
 
 
 def row_orders():
@@ -212,12 +215,20 @@
             for lev in range(2)
         ]
     )
-    cut = one_hot(4 * CELLS, 288, [(quarter_row(k, r, c), k * 72 + r * 12 + c) for k, r, c in cells()])
+    cut = one_hot(
+        4 * PART,
+        144,
+        [
+            (((r // 3) * 2 + c // 6) * PART + k * 18 + (r % 3) * 6 + c % 6, k * 72 + r * 12 + c)
+            for k, r, c in cells()
+            if k < 2
+        ],
+    )
     rolled = one_hot(
-        288, 4 * CELLS, [(k * 72 + r * 12 + c, quarter_row((k + 1) % 4, r, c)) for k, r, c in cells()]
+        288, 8 * PART, [(k * 72 + r * 12 + c, quarter_row((k + 1) % 4, r, c)) for k, r, c in cells()]
     )
     back = one_hot(
-        288, 4 * CELLS, [(r * 48 + c * 4 + (k + 1) % 4, quarter_row(k, r, c)) for k, r, c in cells()]
+        288, 8 * PART, [(r * 48 + c * 4 + (k + 1) % 4, quarter_row(k, r, c)) for k, r, c in cells()]
     )
     return [a.astype(BF) for a in (halves, cut, rolled, back)]
 
@@ -230,6 +241,13 @@
 def pick_head(shape, j):
     lane = lax.broadcasted_iota(jnp.int32, shape, 1)
     return (lane >= j * HD) & (lane < (j + 1) * HD)
+
+
+def region_bias(ids):
+    kinds = lax.broadcasted_iota(jnp.int32, (8, 144), 0)
+    hot = (kinds == jnp.broadcast_to(ids, (8, 144))).astype(F32).astype(BF)
+    bias = jnp.where(dot(hot, hot, ((0,), (0,))) > 0.5, 0.0, -1e30)
+    return jnp.concatenate([bias] * 4, 1)
 
 
 def attention(q, k, v, mask):
@@ -241,7 +259,7 @@
         qs = jnp.concatenate([jnp.where(h, qg, jnp.zeros_like(qg)) for h in heads], 0)
         score = dot(kg, qs, ((1,), (1,)))
         if mask is not None:
-            score = jnp.where(mask, score, -1e30)
+            score = score + mask
         top = jnp.max(score, 0, keepdims=True)
         weight = jnp.exp2((score - top) * EXP_SCALE)
         weight = (weight * (1.0 / jnp.sum(weight, 0, keepdims=True))).astype(BF)
@@ -270,14 +288,7 @@
 
     def window(self, qkv, w, regions=None):
         q, k, v = [part[w * 144 : (w + 1) * 144] for part in qkv]
-        mask = None
-        if regions is not None:
-            kinds = lax.broadcasted_iota(jnp.int32, (8, 144), 0)
-            ids = jnp.broadcast_to(regions[w], (8, 144))
-            hot = (kinds == ids).astype(F32).astype(BF)
-            same = dot(hot, hot, ((0,), (0,)))
-            mask = jnp.concatenate([same] * 4, 1) > 0.5
-        return attention(q, k, v, mask)
+        return attention(q, k, v, None if regions is None else regions[w])
 
     def mix(self, x, context):
         added = [dot(context, self.tile(1, h, 512, 768)) for h in range(2)]
@@ -303,15 +314,20 @@
         return (mixed + jnp.concatenate(sums, 1)).astype(BF)
 
 
-def moved(send_buf, recv_buf, sems, slot, peer, quarter):
+def moved(send_buf, recv_buf, sems, w, slot, peer, quarter):
     return pltpu.make_async_remote_copy(
-        src_ref=send_buf.at[quarter],
-        dst_ref=recv_buf.at[slot],
-        send_sem=sems[0].at[slot],
-        recv_sem=sems[1].at[slot],
+        src_ref=send_buf.at[w, quarter],
+        dst_ref=recv_buf.at[slot, w],
+        send_sem=sems[0].at[slot, w],
+        recv_sem=sems[1].at[slot, w],
         device_id=peer,
         device_id_type=MESH,
     )
+
+
+def tiles_of(own, quarter, received):
+    parts = [own[w, quarter].reshape(PART, D) for w in range(2)]
+    return parts, [received[slot].reshape(2 * PART, D) for slot in range(3)]
 
 
 def kernel(
@@ -428,6 +444,7 @@
     pl.semaphore_wait(barrier, count)
 
     g.start(None, (0, 1, 2))
+    g.start(1, (15, 16, 17))
     loaded(4, 7)
     select = halves[lev]
     for slot in range(4):
@@ -462,11 +479,13 @@
         return score.reshape(4, CELLS, Q_LAT * HEADS), kv[:, D : 2 * D].astype(F32).reshape(4, CELLS, D)
 
     g.step(None, (0, 1, 2), ())
-    g.start(0, (0, 1, 2))
+    g.start(0, (15, 16, 17, 0, 1, 2))
     toks[1].start()
     score_own, val_own = keys_values(tok_own)
-    g.step(0, (0, 1, 2), (3, 4, 5))
-    g.start(0, (7, 9, 8, 10))
+    g.step(0, (15, 16, 17), (3, 4, 5))
+    g.wait(0, (0, 1, 2))
+    g.start(0, (7, 9, 8, 10, 13))
+    g.wait(1, (15, 16, 17))
     g.start(1, (0, 1, 2))
     toks[0].wait_recv()
     toks[1].wait_recv()
@@ -496,38 +515,42 @@
     g.step(0, (7, 9), (11, 12))
     qkv = block.qkv(x)
     context = [block.window(qkv, 0)]
-    g.step(0, (8, 10), (13,))
+    g.step(0, (8, 10), (18, 19))
     g.step(1, (0, 1, 2), (3, 4, 5))
-    g.start(1, (7, 9, 8, 10))
+    g.start(1, (7, 9, 8, 10, 13))
     context.append(block.window(qkv, 1))
-    context = jnp.concatenate(context, 0)
     g.step(0, (11, 12), (14,))
     g.drain(None, (0, 1, 2))
-    g.drain(0, (0, 1, 2, 3, 4, 5, 6))
+    g.drain(0, (0, 1, 2, 3, 4, 5, 6, 15, 16, 17))
     placed = dot(regions[0].astype(F32).astype(BF), columns[0])
     for r in range(1, 6):
         placed = placed + dot(regions[r].astype(F32).astype(BF), columns[r])
     ids = placed.astype(jnp.int32)
     labels = [jnp.concatenate([ids[2 * w : 2 * w + 1], ids[2 * w + 1 : 2 * w + 2]], 1) for w in range(2)]
+    labels = [region_bias(label) for label in labels]
     loaded(16, 19)
-    g.wait(0, (13, 14))
-    mixed = block.mix(x, context)
-    plain = block.feed(mixed)
-    hs[...] = dot(cut[...], plain).reshape(4, TILES, 8, D).astype(BF)
+    g.wait(0, (13, 18, 19, 14))
     sems = (hsem, hrsem)
-    sent = [
-        moved(hs, hr, sems, 1, (lev, behind), 1),
-        moved(hs, hr, sems, 0, partner, 2),
-        moved(hs, hr, sems, 2, (1 - lev, behind), 0),
-    ]
-    for copy in sent:
-        copy.start()
+    sent = []
+    for w in range(2):
+        mixed = block.mix(x[w * 144 : (w + 1) * 144], context[w])
+        plain = block.feed(mixed)
+        hs[w] = dot(cut[...], plain).reshape(4, PART // 8, 8, D).astype(BF)
+        now = [
+            moved(hs, hr, sems, w, 1, (lev, behind), 1),
+            moved(hs, hr, sems, w, 0, partner, 2),
+            moved(hs, hr, sems, w, 2, (1 - lev, behind), 0),
+        ]
+        for copy in now:
+            copy.start()
+        sent += now
+    g.step(1, (7, 9), (11, 12))
     g.step(1, (3, 4, 5), (6,))
-    g.step(1, (7, 9), (11, 12))
-    g.step(1, (8, 10), (13,))
+    g.step(1, (8, 10), (18, 19))
     for copy in sent:
         copy.wait_recv()
-    tiles = jnp.concatenate([part.reshape(CELLS, D) for part in (hs[3], hr[0], hr[1], hr[2])], 0)
+    own, others = tiles_of(hs, 3, hr)
+    tiles = jnp.concatenate(own + others, 0)
     x = dot(roll_rows[...], tiles)
     g.wait(1, (6,))
 
@@ -536,28 +559,31 @@
     context = [block.window(qkv, 0, labels)]
     g.step(1, (11, 12), (14,))
     context.append(block.window(qkv, 1, labels))
-    context = jnp.concatenate(context, 0)
-    g.wait(1, (13, 14))
-    mixed = block.mix(x, context)
-    shifted = block.feed(mixed)
-    hs2[...] = dot(cut[...], shifted).reshape(4, TILES, 8, D).astype(BF)
+    g.wait(1, (13, 18, 19, 14))
     sems = (h2sem, h2rsem)
-    back = [
-        moved(hs2, hr2, sems, 1, (lev, ahead), 2),
-        moved(hs2, hr2, sems, 0, partner, 1),
-        moved(hs2, hr2, sems, 2, (1 - lev, ahead), 3),
-    ]
-    for copy in back:
-        copy.start()
+    back = []
+    for w in range(2):
+        mixed = block.mix(x[w * 144 : (w + 1) * 144], context[w])
+        shifted = block.feed(mixed)
+        hs2[w] = dot(cut[...], shifted).reshape(4, PART // 8, 8, D).astype(BF)
+        now = [
+            moved(hs2, hr2, sems, w, 1, (lev, ahead), 2),
+            moved(hs2, hr2, sems, w, 0, partner, 1),
+            moved(hs2, hr2, sems, w, 2, (1 - lev, ahead), 3),
+        ]
+        for copy in now:
+            copy.start()
+        back += now
     for tok in toks:
         tok.wait_send()
-    g.drain(0, (7, 8, 9, 10, 11, 12, 13, 14))
+    g.drain(0, (7, 8, 9, 10, 11, 12, 13, 14, 18, 19))
     g.drain(1, range(SLOTS))
     for copy in sent:
         copy.wait_send()
     for copy in back:
         copy.wait_recv()
-    tiles = jnp.concatenate([part.reshape(CELLS, D) for part in (hr2[2], hr2[1], hr2[0], hs2[0])], 0)
+    own, others = tiles_of(hs2, 0, hr2)
+    tiles = jnp.concatenate(others[::-1] + own, 0)
     out[...] = dot(back_rows[...], tiles).astype(BF)
     for copy in back:
         copy.wait_send()
@@ -612,15 +638,16 @@
         out_specs=pl.BlockSpec(memory_space=pltpu.VMEM),
         scratch_shapes=[buf(a.shape, a.dtype) for a in operands]
         + [buf((2, 2, 4, 4, 2, 2, 8, width), BF) for width in WIDTHS]
-        + [buf((n, TILES, 8, D), BF) for n in (4, 4, 4, 4, 3, 4, 3)]
+        + [buf((4, TILES, 8, D), BF)] * 3
+        + [buf(lead + (PART // 8, 8, D), BF) for lead in ((2, 4), (3, 2)) * 2]
         + [
             dma((3, 3 + 2 * SLOTS)),
             dma((3, 3 + 2 * SLOTS)),
             dma((4,)),
-            dma((3,)),
-            dma((3,)),
-            dma((3,)),
-            dma((3,)),
+            dma((3, 2)),
+            dma((3, 2)),
+            dma((3, 2)),
+            dma((3, 2)),
             dma((len(operands),)),
         ],
         compiler_params=pltpu.CompilerParams(

time: 61.3 us -> 60.8 us (level)
  no operation moved by 1% of the time
where the time goes in v5:
time: 60.8 us; the launch traced here: 60.7 us
  Pallas kernels  58.9 us (97%)
  local copies, waits for them, and re-layouts  1.75 us (3%)
    pallas_call x1, Pallas kernels, local(): pl.pallas_call(kernel, out_shape=jax.ShapeDtypeStruct((288, D), BF), in_s...  58.9 us
    reshape x1, local copies, waits for them, and re-layouts, local(): return flat.reshape(6, 12, Q_LAT, D)  1.75 us

profile of v5, /device:TPU:0, one launch (start us, length us, event | category | flops | bytes accessed | tf_op | source)
XLA Modules:
  0.0 60.7 jit_solution(1178182829098385592)
XLA Ops:
  0.0 58.9 %encode_and_blocks.1 = bf16[288,512]{1,0:T(8,128)(2,1)} custom-call(s32[4]{0:T(128)} %level_ids.1, f32[13,512]{1,0:T(8,128)} %level_table_h.1, bf16[4,512]{1,0:T(4,128)(2,1)} %latent_query_h.1, s32[6,4,12]{2,1,0:T(4,128)} %bitcast.1, f32[2,512]{1,0:T(2,128)} %gain_one_h.1, f32[2,512]{1,0:T(2,128)} %gain_two_h.1, bf16[4,6,24,512]{3,2,1,0:T(8,128)(2,1)} %tokens_h.1, ...), custom_call_target="tpu_custom_call" | custom-call | tf_op jit(solution)/shard_map/encode_and_blocks/pallas_call | solution.py:633
  58.9 1.7 %reshape.3 = bf16[6,12,4,512]{3,2,1,0:T(4,128)(2,1)} reshape(bf16[288,512]{1,0:T(8,128)(2,1)} %encode_and_blocks.1) | data formatting | bytes 589824 | tf_op jit(solution)/shard_map/reshape | solution.py:658

commit v6 on v5

--- a/solution.py
+++ b/solution.py
@@ -350,7 +350,6 @@
     columns_h,
     cut_h,
     roll_rows_h,
-    back_rows_h,
     out,
     level_table,
     latent_query,
@@ -370,7 +369,6 @@
     columns,
     cut,
     roll_rows,
-    back_rows,
     ba,
     bb,
     bc,
@@ -414,7 +412,6 @@
         (columns_h, columns),
         (cut_h, cut),
         (roll_rows_h, roll_rows),
-        (back_rows_h, back_rows),
     )
     loads = [pltpu.make_async_copy(src, dst, load_sem.at[n]) for n, (src, dst) in enumerate(pairs)]
     for load in loads:
@@ -528,7 +525,7 @@
     ids = placed.astype(jnp.int32)
     labels = [jnp.concatenate([ids[2 * w : 2 * w + 1], ids[2 * w + 1 : 2 * w + 2]], 1) for w in range(2)]
     labels = [region_bias(label) for label in labels]
-    loaded(16, 19)
+    loaded(16, 18)
     g.wait(0, (13, 18, 19, 14))
     sems = (hsem, hrsem)
     sent = []
@@ -546,7 +543,6 @@
         sent += now
     g.step(1, (7, 9), (11, 12))
     g.step(1, (3, 4, 5), (6,))
-    g.step(1, (8, 10), (18, 19))
     for copy in sent:
         copy.wait_recv()
     own, others = tiles_of(hs, 3, hr)
@@ -556,6 +552,7 @@
 
     block = Block(1, bufs, gain_one, gain_two)
     qkv = block.qkv(x)
+    g.step(1, (8, 10), (18, 19))
     context = [block.window(qkv, 0, labels)]
     g.step(1, (11, 12), (14,))
     context.append(block.window(qkv, 1, labels))
@@ -583,10 +580,13 @@
     for copy in back:
         copy.wait_recv()
     own, others = tiles_of(hs2, 0, hr2)
-    tiles = jnp.concatenate(others[::-1] + own, 0)
-    out[...] = dot(back_rows[...], tiles).astype(BF)
+    out[...] = jnp.concatenate(others[::-1] + own, 0)
     for copy in back:
         copy.wait_send()
+
+
+def in_order(order, tiles, out):
+    out[...] = dot(order[...], tiles[...]).reshape(CELLS, Q_LAT, D).astype(BF)
 
 
 def local(
@@ -626,13 +626,12 @@
         jnp.asarray(place_row.astype(BF)),
         cut,
         roll_rows,
-        back_rows,
     )
     buf = pltpu.VMEM
     dma = pltpu.SemaphoreType.DMA
     flat = pl.pallas_call(
         kernel,
-        out_shape=jax.ShapeDtypeStruct((288, D), BF),
+        out_shape=jax.ShapeDtypeStruct((8 * PART, D), BF),
         in_specs=[pl.BlockSpec(memory_space=pltpu.SMEM)]
         + [pl.BlockSpec(memory_space=pl.ANY)] * len(operands),
         out_specs=pl.BlockSpec(memory_space=pltpu.VMEM),
@@ -655,6 +654,14 @@
         ),
         name="encode_and_blocks",
     )(level_ids, *operands)
+    vmem = pl.BlockSpec(memory_space=pltpu.VMEM)
+    flat = pl.pallas_call(
+        in_order,
+        out_shape=jax.ShapeDtypeStruct((CELLS, Q_LAT, D), BF),
+        in_specs=[vmem, vmem],
+        out_specs=vmem,
+        name="final_order",
+    )(back_rows, flat)
     return flat.reshape(6, 12, Q_LAT, D)
 
 

time: 60.8 us -> 60.8 us (level)
  Pallas kernels: 58.9 us -> 60.7 us
  local copies, waits for them, and re-layouts: 1.75 us -> 0 us
    pallas_call x1 -> x2, Pallas kernels: 58.9 us -> 60.7 us  [the longest x1 58.6 us: local(): pl.pallas_call(kernel, out_shape=jax.ShapeDtypeStruct((8 * PART, D), BF),...]
    reshape x1 -> x0, local copies, waits for them, and re-layouts: 1.75 us -> none  [local(): return flat.reshape(6, 12, Q_LAT, D)]
where the time goes in v6:
time: 60.8 us; the launch traced here: 60.7 us
  Pallas kernels  60.7 us (100%)
    pallas_call x1, Pallas kernels, local(): pl.pallas_call(kernel, out_shape=jax.ShapeDtypeStruct((8 * PART, D), BF),...  58.6 us
    pallas_call x1, Pallas kernels, local(): pl.pallas_call(in_order, out_shape=jax.ShapeDtypeStruct((CELLS, Q_LAT, D)...  2.14 us

profile of v6, /device:TPU:0, one launch (start us, length us, event | category | flops | bytes accessed | tf_op | source)
XLA Modules:
  0.0 60.7 jit_solution(10574899074411042094)
XLA Ops:
  0.0 58.6 %encode_and_blocks.1.tiles = bf16[320,512]{1,0:T(8,128)(2,1)} custom-call(s32[4]{0:T(128)} %level_ids.1, f32[13,512]{1,0:T(8,128)} %level_table_h.1, bf16[4,512]{1,0:T(4,128)(2,1)} %latent_query_h.1, s32[6,4,12]{2,1,0:T(4,128)} %bitcast.2, f32[2,512]{1,0:T(2,128)} %gain_one_h.1, f32[2,512]{1,0:T(2,128)} %gain_two_h.1, bf16[4,6,24,512]{3,2,1,0:T(8,128)(2,1)} %tokens_h.1, ...), custom_call_target="tpu_custom_call" | custom-call | tf_op jit(solution)/shard_map/encode_and_blocks/pallas_call | solution.py:632
  58.6 2.1 %final_order.1 = bf16[72,4,512]{2,1,0:T(4,128)(2,1)} custom-call(bf16[288,320]{1,0:T(8,128)(2,1)} %constant.15.clone.order, bf16[320,512]{1,0:T(8,128)(2,1)} %encode_and_blocks.1.tiles), custom_call_target="tpu_custom_call" | custom-call | tf_op jit(solution)/shard_map/final_order/pallas_call | solution.py:658
